TPU v7x, 32 devices: a whole 2x2x4 slice. The times are simulated.
32 devices in a mesh: seq: 8 (over z, y), fsdp: 4 (over x, core).
Axes of the slice: x: 2, y: 2, z: 4, core: 2. Of those that a mesh axis runs over, the one named last changes fastest.
Arguments:
- features: bfloat16 [2, 4, 2048, 512], P(None, 'fsdp', 'seq'), may hold values from -6 to 6
- lengths: int32 [2, 4, 12], P(None, 'fsdp'), may hold values from 1 to 896, as said below
- conv_weight: bfloat16 [1536, 512], P(('seq', 'fsdp')), may hold values from -0.15625 to 0.15625
- feature_gain: bfloat16 [512], P(('seq', 'fsdp')), may hold values from 0.25 to 1.75
- projection_weight: bfloat16 [512, 768], P(('seq', 'fsdp')), may hold values from -0.25 to 0.25
- position_weight: bfloat16 [6144, 768], P(('seq', 'fsdp')), may hold values from -0.078125 to 0.078125
- encoder_gain: bfloat16 [768], P(('seq', 'fsdp')), may hold values from 0.25 to 1.75
- qkv_weight: bfloat16 [768, 2304], P(('seq', 'fsdp')), may hold values from -0.21875 to 0.21875
- output_weight: bfloat16 [768, 768], P(('seq', 'fsdp')), may hold values from -3.5 to 3.5
- attention_gain: bfloat16 [768], P(('seq', 'fsdp')), may hold values from 0.25 to 1.75
- up_weight: bfloat16 [768, 3072], P(('seq', 'fsdp')), may hold values from -0.21875 to 0.21875
- down_weight: bfloat16 [3072, 768], P(('seq', 'fsdp')), may hold values from -0.109375 to 0.109375
- final_gain: bfloat16 [768], P(('seq', 'fsdp')), may hold values from 0.25 to 1.75
- cotangent: bfloat16 [2, 4, 1024, 768], P(None, 'fsdp', 'seq'), may hold values from -6 to 6
Outputs:
- block_output: float32 [2, 4, 1024, 768], P(None, 'fsdp', 'seq')
- feature_grad: float32 [2, 4, 2048, 512], P(None, 'fsdp', 'seq')
- conv_weight_grad: float32 [1536, 512], P(('seq', 'fsdp'))
- feature_gain_grad: float32 [512], P(('seq', 'fsdp'))
- projection_weight_grad: float32 [512, 768], P(('seq', 'fsdp'))
- position_weight_grad: float32 [6144, 768], P(('seq', 'fsdp'))
- encoder_gain_grad: float32 [768], P(('seq', 'fsdp'))
- qkv_weight_grad: float32 [768, 2304], P(('seq', 'fsdp'))
- output_weight_grad: float32 [768, 768], P(('seq', 'fsdp'))
- attention_gain_grad: float32 [768], P(('seq', 'fsdp'))
- up_weight_grad: float32 [768, 3072], P(('seq', 'fsdp'))
- down_weight_grad: float32 [3072, 768], P(('seq', 'fsdp'))
- final_gain_grad: float32 [768], P(('seq', 'fsdp'))
Inputs may be any that keep to these rules, and one draw needn't show every extreme that they name: For each micro-batch and stream, 12 utterance lengths in output frames, in order along the stream, summing to 1024.
All inputs are finite; a program needn't handle non-finite values.
Results may differ from a plain program's by a relative error of at most 0.023.
Values may be sent and summed in bfloat16 or wider, within the bound.
No kernel may reach another device: no remote copies, remote signals or barrier semaphores. Data moves between devices by JAX's collectives and lax.ppermute only.
A program may use at most 320 MiB of HBM per device.

v0:
```python
import math

import jax
import jax.numpy as jnp
import numpy as np
from jax import lax
from jax.experimental import pallas as pl
from jax.experimental.pallas import tpu as pltpu
from jax.sharding import PartitionSpec as P

D = 768
HEADS = 12
C_CNN = 512
POS_K = 128
GROUPS = 16
HEAD_DIM = 64
CG = 48
HALF = POS_K // 2
FINE = 16
COARSE = POS_K // FINE
HEAD_PARTS = 4
MICROS = 2
LOG2E = 1.4426950408889634
VMEM = 60 * 1024 * 1024

NORM_EPS = 1e-05
F32 = jnp.float32
BF16 = jnp.bfloat16


def shifted(array, axis, by):
    peers = lax.axis_size(axis)
    pairs = [(i, i + by) for i in range(peers) if 0 <= i + by < peers]
    return lax.ppermute(array, axis, pairs)


def flip(blocks, me):
    count = len(blocks)
    return [lax.select_n(me, *(blocks[m ^ k] for m in range(count))) for k in range(count)]


def swapped(array, k):
    count = lax.axis_size("fsdp")
    return lax.ppermute(array, "fsdp", [(i, i ^ k) for i in range(count)])


def swap_parts(parts, me):
    ordered = flip(parts, me)
    return flip([ordered[0]] + [swapped(ordered[k], k) for k in range(1, 4)], me)


def gather_blocks(block):
    over_x = swapped(block, 2)
    return [block, swapped(block, 1), over_x, swapped(over_x, 1)]


def after(value, other):
    return lax.optimization_barrier((value, other))[0]


def low_sum(*terms):
    return sum(term.astype(F32) for term in terms).astype(BF16)


def pair_sums(blocks):
    return low_sum(blocks[0], swapped(blocks[1], 1)), low_sum(blocks[2], swapped(blocks[3], 1))


def reduce_blocks(blocks):
    kept, sent = pair_sums(blocks)
    return low_sum(kept, swapped(sent, 2))


def norm_rows(values, scales):
    center = values - jnp.mean(values, axis=-1, keepdims=True)
    spread = jnp.mean(center * center, axis=-1, keepdims=True)
    return center * lax.rsqrt(spread + NORM_EPS) * scales


def smooth_gate(values):
    return jax.nn.gelu(values, approximate=False)


def segment_of(utterance_ends, positions):
    return jnp.sum(
        (utterance_ends[..., None, :] <= positions[:, None]).astype(jnp.int32),
        axis=-1,
        dtype=jnp.int32,
    )


def plain_dot(left, right):
    return jnp.dot(left, right, preferred_element_type=F32)


def inner_dot(left, right):
    return lax.dot_general(left, right, (((0,), (0,)), ((), ())), preferred_element_type=F32)


def outer_dot(left, right):
    return lax.dot_general(left, right, (((1,), (1,)), ((), ())), preferred_element_type=F32)


def lane_roll(value, shift):
    shift = shift % value.shape[1]
    return pltpu.roll(value, shift, 1) if shift else value


def joined(ref, edge_ref, micro, frames):
    columns = slice(micro * frames, (micro + 1) * frames)
    edge = slice(micro * POS_K, (micro + 1) * POS_K)
    blocks = [ref[s, :, columns] for s in range(ref.shape[0])] + [edge_ref[:, edge]]
    return jnp.concatenate(blocks, axis=1).astype(F32)


def fine_shifts(x_ref, edge_ref, fine_ref, frames, span):
    for m in range(MICROS):
        x = joined(x_ref, edge_ref, m, frames)
        for fine in range(FINE):
            fine_ref[fine * CG : (fine + 1) * CG, m * span : (m + 1) * span] = lane_roll(
                x, HALF - fine
            ).astype(BF16)


def store_frames(out_ref, micro, frames, total):
    for s in range(out_ref.shape[0]):
        out_ref[s, :, micro * frames : (micro + 1) * frames] = total[
            :, s * frames : (s + 1) * frames
        ].astype(BF16)


def position_kernel(span, frames, x_ref, edge_ref, w_ref, out_ref, fine_ref):
    fine_shifts(x_ref, edge_ref, fine_ref, frames, span)
    weights = w_ref[...].reshape(COARSE * CG, FINE * CG)
    for m in range(MICROS):
        terms = jnp.dot(
            weights, fine_ref[:, m * span : (m + 1) * span], preferred_element_type=F32
        )
        total = terms[:CG]
        for coarse in range(1, COARSE):
            total += lane_roll(terms[coarse * CG : (coarse + 1) * CG], -FINE * coarse)
        store_frames(out_ref, m, frames, total)


def position_back_kernel(
    span, frames, x_ref, x_edge_ref, g_ref, g_edge_ref, w_ref, dx_ref, dw_ref,
    fine_ref, coarse_ref, own_ref,
):
    fine_shifts(x_ref, x_edge_ref, fine_ref, frames, span)
    column = lax.broadcasted_iota(jnp.int32, (CG, span), 1)
    for m in range(MICROS):
        columns = slice(m * span, (m + 1) * span)
        g = joined(g_ref, g_edge_ref, m, frames)
        own = jnp.where(column < span - POS_K, g, 0.0)
        for coarse in range(COARSE):
            rows = slice(coarse * CG, (coarse + 1) * CG)
            back = FINE * (COARSE - 1 - coarse)
            coarse_ref[rows, columns] = lane_roll(g, HALF - back).astype(BF16)
            own_ref[rows, columns] = lane_roll(own, FINE * coarse).astype(BF16)
    weights = w_ref[...].reshape(COARSE * CG, FINE * CG)
    turned = weights.astype(F32).T.astype(BF16)
    for m in range(MICROS):
        terms = jnp.dot(
            turned, coarse_ref[:, m * span : (m + 1) * span], preferred_element_type=F32
        )
        total = lane_roll(terms[:CG], -FINE)
        for fine in range(1, FINE):
            total += lane_roll(terms[fine * CG : (fine + 1) * CG], fine - FINE)
        store_frames(dx_ref, m, frames, total)
    grad = lax.dot_general(
        own_ref[...], fine_ref[...], (((1,), (1,)), ((), ())), preferred_element_type=F32
    )
    dw_ref[...] = grad.astype(BF16).reshape(COARSE, CG, FINE * CG)


def group_specs(count, columns):
    wide = pl.BlockSpec((count, CG, columns), lambda g: (0, g, 0))
    edge = pl.BlockSpec((CG, MICROS * POS_K), lambda g: (g, 0))
    weight = pl.BlockSpec((COARSE, CG, FINE * CG), lambda g: (0, g, 0))
    return wide, edge, weight


def position_conv(x, edge, weights):
    count, channels, columns = x.shape
    frames = columns // MICROS
    span = count * frames + POS_K
    groups = channels // CG
    wide, edge_spec, weight = group_specs(count, columns)
    return pl.pallas_call(
        lambda *refs: position_kernel(span, frames, *refs),
        grid=(groups,),
        in_specs=[wide, edge_spec, weight],
        out_specs=wide,
        out_shape=jax.ShapeDtypeStruct(x.shape, BF16),
        scratch_shapes=[pltpu.VMEM((FINE * CG, MICROS * span), BF16)],
        compiler_params=pltpu.CompilerParams(vmem_limit_bytes=VMEM),
        cost_estimate=pl.CostEstimate(flops=0, bytes_accessed=0, transcendentals=0),
        name="position_conv",
    )(x, edge, weights)


def position_back(x, x_edge, grad, grad_edge, weights):
    count, channels, columns = x.shape
    frames = columns // MICROS
    span = count * frames + POS_K
    groups = channels // CG
    wide, edge_spec, weight = group_specs(count, columns)
    return pl.pallas_call(
        lambda *refs: position_back_kernel(span, frames, *refs),
        grid=(groups,),
        in_specs=[wide, edge_spec, wide, edge_spec, weight],
        out_specs=[wide, weight],
        out_shape=[
            jax.ShapeDtypeStruct(x.shape, BF16),
            jax.ShapeDtypeStruct(weights.shape, BF16),
        ],
        scratch_shapes=[
            pltpu.VMEM((FINE * CG, MICROS * span), BF16),
            pltpu.VMEM((COARSE * CG, MICROS * span), BF16),
            pltpu.VMEM((COARSE * CG, MICROS * span), BF16),
        ],
        compiler_params=pltpu.CompilerParams(vmem_limit_bytes=VMEM),
        cost_estimate=pl.CostEstimate(flops=0, bytes_accessed=0, transcendentals=0),
        name="position_back",
    )(x, x_edge, grad, grad_edge, weights)


def side_by_side(ref):
    return jnp.concatenate([ref[s, 0] for s in range(ref.shape[0])], axis=1)


def turn(value):
    return value.astype(F32).T.astype(BF16)


def attention_kernel(block, q_ref, k_ref, v_ref, seg_q_ref, seg_k_ref, out_ref):
    queries = turn(side_by_side(q_ref))
    keys = side_by_side(k_ref)
    values = side_by_side(v_ref)
    frames = out_ref.shape[2]
    factor = HEAD_DIM**-0.5 * LOG2E
    for first in range(0, queries.shape[0], block):
        rows = slice(first, first + block)
        scores = jnp.dot(queries[rows], keys, preferred_element_type=F32)
        expo = jnp.where(seg_q_ref[rows] == seg_k_ref[...], jnp.exp2(scores * factor), 0.0)
        weight_sum = jnp.sum(expo, axis=1, keepdims=True)
        accum = lax.dot_general(
            expo.astype(BF16), values, (((1,), (1,)), ((), ())), preferred_element_type=F32
        )
        context = (accum / weight_sum).T
        for part in range(block // frames):
            out_ref[first // frames + part] = context[:, part * frames : (part + 1) * frames]


def attention_back_kernel(
    block, q_ref, k_ref, v_ref, cg_ref, ctx_ref, seg_q_ref, seg_k_ref,
    dq_ref, dk_ref, dv_ref, dk_sum, dv_sum,
):
    keys_across = side_by_side(k_ref)
    keys = turn(keys_across)
    values = turn(side_by_side(v_ref))
    frames = ctx_ref.shape[2]
    parts = block // frames
    scale = HEAD_DIM**-0.5
    for step in range(q_ref.shape[0] // parts):
        some = range(step * parts, (step + 1) * parts)
        columns = slice(step * block, (step + 1) * block)
        queries = jnp.concatenate([q_ref[s, 0] for s in some], axis=1)
        context_grad = jnp.concatenate([cg_ref[s].astype(F32) for s in some], axis=1)
        context = jnp.concatenate([ctx_ref[s] for s in some], axis=1)
        scores = jnp.dot(keys, queries, preferred_element_type=F32)
        expo = jnp.where(
            seg_k_ref[...] == seg_q_ref[:, columns], jnp.exp2(scores * (scale * LOG2E)), 0.0
        )
        inverse = 1.0 / jnp.sum(expo, axis=0, keepdims=True)
        accum_g = (context_grad * inverse).astype(BF16)
        correction = jnp.sum(context_grad * context, axis=0, keepdims=True) * inverse
        dots = jnp.dot(values, accum_g, preferred_element_type=F32)
        score_g = (expo * (dots - correction)).astype(BF16)
        query_grad = jnp.dot(keys_across, score_g, preferred_element_type=F32) * scale
        for part, s in enumerate(some):
            dq_ref[s] = query_grad[:, part * frames : (part + 1) * frames].astype(BF16)
        key_grad = lax.dot_general(
            score_g, queries, (((1,), (1,)), ((), ())), preferred_element_type=F32
        )
        value_grad = lax.dot_general(
            expo.astype(BF16), accum_g, (((1,), (1,)), ((), ())), preferred_element_type=F32
        )
        if step == 0:
            dk_sum[...] = key_grad
            dv_sum[...] = value_grad
        else:
            dk_sum[...] += key_grad
            dv_sum[...] += value_grad
    key_total = (dk_sum[...] * scale).T.astype(BF16)
    value_total = dv_sum[...].T.astype(BF16)
    for s in range(dk_ref.shape[0]):
        dk_ref[s] = key_total[:, s * frames : (s + 1) * frames]
        dv_ref[s] = value_total[:, s * frames : (s + 1) * frames]


def head_spec(count, frames, which):
    return pl.BlockSpec((count, 1, HEAD_DIM, frames), lambda h: (0, which, h, 0))


def plain_spec(count, frames):
    return pl.BlockSpec((count, HEAD_DIM, frames), lambda h: (0, h, 0))


def whole_spec(array):
    return pl.BlockSpec(array.shape, lambda h: (0,) * array.ndim)


def attention(mixed, mixed_all, seg_q, seg_k):
    count, _, channels, frames = mixed.shape
    total = mixed_all.shape[0]
    heads = channels // HEAD_DIM
    block = math.gcd(count, 2) * frames
    seg_q, seg_k = seg_q[:, None], seg_k[None]
    return pl.pallas_call(
        lambda *refs: attention_kernel(block, *refs),
        grid=(heads,),
        in_specs=[
            head_spec(count, frames, 0),
            head_spec(total, frames, 1),
            head_spec(total, frames, 2),
            whole_spec(seg_q),
            whole_spec(seg_k),
        ],
        out_specs=plain_spec(count, frames),
        out_shape=jax.ShapeDtypeStruct((count, channels, frames), F32),
        compiler_params=pltpu.CompilerParams(vmem_limit_bytes=VMEM),
        cost_estimate=pl.CostEstimate(flops=0, bytes_accessed=0, transcendentals=0),
        name="attention",
    )(mixed, mixed_all, mixed_all, seg_q, seg_k)


def attention_back(mixed, mixed_all, context_grad, context, seg_q, seg_k):
    count, _, channels, frames = mixed.shape
    total = mixed_all.shape[0]
    heads = channels // HEAD_DIM
    block = math.gcd(count, 2) * frames
    seg_q, seg_k = seg_q[None], seg_k[:, None]
    return pl.pallas_call(
        lambda *refs: attention_back_kernel(block, *refs),
        grid=(heads,),
        in_specs=[
            head_spec(count, frames, 0),
            head_spec(total, frames, 1),
            head_spec(total, frames, 2),
            plain_spec(count, frames),
            plain_spec(count, frames),
            whole_spec(seg_q),
            whole_spec(seg_k),
        ],
        out_specs=[
            plain_spec(count, frames),
            plain_spec(total, frames),
            plain_spec(total, frames),
        ],
        out_shape=[
            jax.ShapeDtypeStruct((count, channels, frames), BF16),
            jax.ShapeDtypeStruct((total, channels, frames), BF16),
            jax.ShapeDtypeStruct((total, channels, frames), BF16),
        ],
        scratch_shapes=[pltpu.VMEM((total * frames, HEAD_DIM), F32)] * 2,
        compiler_params=pltpu.CompilerParams(vmem_limit_bytes=VMEM),
        cost_estimate=pl.CostEstimate(flops=0, bytes_accessed=0, transcendentals=0),
        name="attention_back",
    )(mixed, mixed_all, mixed_all, context_grad, context, seg_q, seg_k)


def gate_and_slope(values):
    inner = 0.5 + 0.5 * lax.erf(values * math.sqrt(0.5))
    density = jnp.exp(-0.5 * values * values) * (1.0 / math.sqrt(2.0 * math.pi))
    return values * inner, inner + values * density


def norm_parts(values):
    center = values - jnp.mean(values, axis=1, keepdims=True)
    spread = jnp.mean(center * center, axis=1, keepdims=True)
    rate = lax.rsqrt(spread + NORM_EPS)
    return center * rate, rate


def norm_back(unit, rate, gain, grad):
    scaled = grad * gain
    level = jnp.mean(scaled, axis=1, keepdims=True)
    slope = jnp.mean(scaled * unit, axis=1, keepdims=True)
    return rate * (scaled - level - unit * slope), jnp.sum(grad * unit, axis=0, keepdims=True)


def dot_nt(left, right):
    return lax.dot_general(left, right, (((1,), (1,)), ((), ())), preferred_element_type=F32)


def feed_kernel(
    ctx_ref, out_w_ref, encoded_ref, attention_gain_ref, final_gain_ref, cotangent_ref,
    feed0, feed1, feed2, feed3,
    block_out_ref, mid_ref, context_grad_ref, attention_grad_ref, final_grad_ref,
    settled_ref, hidden_ref, fed_ref, up_ref, branch_ref,
    weights, slopes, sems,
):
    copies = [
        pltpu.make_async_copy(feed, weights.at[k], sems.at[k])
        for k, feed in enumerate((feed0, feed1, feed2, feed3))
    ]
    for copy in copies:
        copy.start()
    kinds, part, frames = ctx_ref.shape
    heads = kinds // MICROS
    width = weights.shape[1]
    units = weights.shape[2] - width
    context = jnp.concatenate(
        [
            jnp.concatenate([ctx_ref[h * MICROS + m] for m in range(MICROS)], axis=1)
            for h in range(heads)
        ],
        axis=0,
    )
    context = turn(context)
    attention_gain = attention_gain_ref[...]
    final_gain = final_gain_ref[...]
    branch = jnp.dot(context, out_w_ref[...], preferred_element_type=F32)
    unit, rate = norm_parts(encoded_ref[...] + branch)
    settled = unit * attention_gain
    settled_low = settled.astype(BF16)
    settled_ref[...] = settled_low
    fed = settled
    for k, copy in enumerate(copies):
        copy.wait()
        columns = slice(k * units, (k + 1) * units)
        up_values = jnp.dot(settled_low, weights[k, :, :units], preferred_element_type=F32)
        hidden, slope = gate_and_slope(up_values)
        slopes[:, columns] = slope
        hidden_low = hidden.astype(BF16)
        hidden_ref[:, columns] = hidden_low
        fed += jnp.dot(hidden_low, weights[k, :, units:], preferred_element_type=F32)
    final_unit, final_rate = norm_parts(fed)
    block_out_ref[...] = final_unit * final_gain
    sum_grad, final_grad_ref[...] = norm_back(
        final_unit, final_rate, final_gain, cotangent_ref[...].astype(F32)
    )
    fed_low = sum_grad.astype(BF16)
    fed_ref[...] = fed_low
    settled_grad = sum_grad
    for k in range(len(copies)):
        columns = slice(k * units, (k + 1) * units)
        up_low = (dot_nt(fed_low, weights[k, :, units:]) * slopes[:, columns]).astype(BF16)
        up_ref[:, columns] = up_low
        settled_grad += dot_nt(up_low, weights[k, :, :units])
    mid_grad, attention_grad_ref[...] = norm_back(unit, rate, attention_gain, settled_grad)
    mid_ref[...] = mid_grad
    branch_low = mid_grad.astype(BF16)
    branch_ref[...] = branch_low
    context_grad = dot_nt(out_w_ref[...], branch_low).astype(BF16)
    for h in range(heads):
        for m in range(MICROS):
            context_grad_ref[h * MICROS + m] = context_grad[
                h * part : (h + 1) * part, m * frames : (m + 1) * frames
            ]


def feed_forward(context, out_w, encoded, attention_gain, final_gain, cotangent, feeds):
    rows, width = encoded.shape
    units = feeds[0].shape[1] - width
    wide = len(feeds) * units
    vmem = pl.BlockSpec(memory_space=pltpu.VMEM)
    return pl.pallas_call(
        feed_kernel,
        in_specs=[vmem] * 6 + [pl.BlockSpec(memory_space=pl.ANY)] * 4,
        out_specs=[vmem] * 10,
        out_shape=[
            jax.ShapeDtypeStruct((rows, width), F32),
            jax.ShapeDtypeStruct((rows, width), F32),
            jax.ShapeDtypeStruct(context.shape, BF16),
            jax.ShapeDtypeStruct((1, width), F32),
            jax.ShapeDtypeStruct((1, width), F32),
            jax.ShapeDtypeStruct((rows, width), BF16),
            jax.ShapeDtypeStruct((rows, wide), BF16),
            jax.ShapeDtypeStruct((rows, width), BF16),
            jax.ShapeDtypeStruct((rows, wide), BF16),
            jax.ShapeDtypeStruct((rows, width), BF16),
        ],
        scratch_shapes=[
            pltpu.VMEM((len(feeds), width, width + units), BF16),
            pltpu.VMEM((rows, wide), F32),
            pltpu.SemaphoreType.DMA((len(feeds),)),
        ],
        compiler_params=pltpu.CompilerParams(vmem_limit_bytes=VMEM),
        cost_estimate=pl.CostEstimate(flops=0, bytes_accessed=0, transcendentals=0),
        name="feed_forward",
    )(context, out_w, encoded, attention_gain, final_gain, cotangent, *feeds)


def feed_grad_kernel(stream_ref, settled_ref, up_ref, hidden_ref, fed_ref, out_ref):
    stream = stream_ref[0]
    seqs, streams, _, _, rows, width = out_ref.shape
    units = up_ref.shape[1] // streams
    settled = turn(settled_ref[...])
    fed = fed_ref[...]
    for k in range(streams):
        f = k ^ stream
        columns = slice(k * units, (k + 1) * units)
        down_grad = jnp.dot(turn(hidden_ref[:, columns]), fed, preferred_element_type=F32)
        up_grad = jnp.dot(settled, up_ref[:, columns], preferred_element_type=F32)
        for s in range(seqs):
            for j in range(streams):
                first = (s * streams + j) * rows
                piece = slice(first, first + rows)
                out_ref[s, f, 0, j] = down_grad[piece].astype(BF16)
                out_ref[s, j, 1, f] = up_grad[piece].astype(BF16)


def feed_grad(stream, settled, up, hidden, fed, seqs):
    rows, width = settled.shape
    streams = up.shape[1] // width
    vmem = pl.BlockSpec(memory_space=pltpu.VMEM)
    shape = (seqs, streams, 2, streams, width // (seqs * streams), width)
    return pl.pallas_call(
        feed_grad_kernel,
        in_specs=[pl.BlockSpec(memory_space=pltpu.SMEM)] + [vmem] * 4,
        out_specs=vmem,
        out_shape=jax.ShapeDtypeStruct(shape, BF16),
        compiler_params=pltpu.CompilerParams(vmem_limit_bytes=VMEM),
        cost_estimate=pl.CostEstimate(flops=0, bytes_accessed=0, transcendentals=0),
        name="feed_grad",
    )(stream, settled, up, hidden, fed)


def head_kernel(width, encoded_ref, *refs):
    blocks, out_ref = refs[:-1], refs[-1]
    frames = out_ref.shape[2]
    encoded = encoded_ref[...]
    for k, block in enumerate(blocks):
        mixed = jnp.dot(encoded, block[:, :width], preferred_element_type=F32).T.astype(BF16)
        for m in range(MICROS):
            out_ref[k * MICROS + m] = mixed[:, m * frames : (m + 1) * frames]


def head_projection(encoded, blocks, width):
    rows, depth = encoded.shape
    vmem = pl.BlockSpec(memory_space=pltpu.VMEM)
    shape = (len(blocks) * MICROS, width, rows // MICROS)
    return pl.pallas_call(
        lambda *refs: head_kernel(width, *refs),
        in_specs=[vmem] * (1 + len(blocks)),
        out_specs=vmem,
        out_shape=jax.ShapeDtypeStruct(shape, BF16),
        compiler_params=pltpu.CompilerParams(vmem_limit_bytes=VMEM),
        cost_estimate=pl.CostEstimate(flops=0, bytes_accessed=0, transcendentals=0),
        name="head_projection",
    )(encoded, *blocks)


def head_back_kernel(
    width, mixed_ref, mid_ref, position_ref, projected_ref, gain_ref, block0, block1, block2,
    block3, joined_ref, position_grad_ref, gain_grad_ref,
):
    total = mid_ref[...]
    for k, block in enumerate((block0, block1, block2, block3)):
        pieces = [mixed_ref[k * MICROS + m].astype(F32).T for m in range(MICROS)]
        mixed = jnp.concatenate(pieces, axis=0).astype(BF16)
        total += dot_nt(mixed, block[:, :width])
    position, slope = gate_and_slope(position_ref[...].astype(F32).T)
    unit, rate = norm_parts(projected_ref[...] + position)
    joined, gain_grad_ref[...] = norm_back(unit, rate, gain_ref[...], total)
    joined_ref[...] = joined
    position_grad_ref[...] = (joined * slope).T.astype(BF16)


def head_back(mixed, mid_grad, position, projected, gain, blocks, width):
    rows, depth = mid_grad.shape
    vmem = pl.BlockSpec(memory_space=pltpu.VMEM)
    return pl.pallas_call(
        lambda *refs: head_back_kernel(width, *refs),
        in_specs=[vmem] * (5 + len(blocks)),
        out_specs=[vmem] * 3,
        out_shape=[
            jax.ShapeDtypeStruct((rows, depth), F32),
            jax.ShapeDtypeStruct((depth, rows), BF16),
            jax.ShapeDtypeStruct((1, depth), F32),
        ],
        compiler_params=pltpu.CompilerParams(vmem_limit_bytes=VMEM),
        cost_estimate=pl.CostEstimate(flops=0, bytes_accessed=0, transcendentals=0),
        name="head_back",
    )(mixed, mid_grad, position, projected, gain, *blocks)


def front_kernel(
    stream_ref, back_ref, joined_ref, normed_ref, projection_ref, before_ref, feature_gain_ref,
    unfolded_ref, conv_ref, encoder_ref, attention_ref, final_ref, mask_n_ref, mask_w_ref,
    place0, place1, place2, place3, packed_ref, unfolded_grad_ref,
):
    stream = stream_ref[0]
    projected_grad = (joined_ref[...] + back_ref[...].astype(F32).T).astype(BF16)
    normed_grad = dot_nt(projected_grad, projection_ref[...])
    activated, slope = gate_and_slope(before_ref[...])
    unit, rate = norm_parts(activated)
    activated_grad, feature_grad = norm_back(unit, rate, feature_gain_ref[...], normed_grad)
    before_low = (activated_grad * slope).astype(BF16)
    unfolded_grad_ref[...] = dot_nt(before_low, conv_ref[...])
    conv_grad = jnp.dot(turn(unfolded_ref[...]), before_low, preferred_element_type=F32)
    projection_grad = jnp.dot(turn(normed_ref[...]), projected_grad, preferred_element_type=F32)
    gains = jnp.zeros((mask_n_ref.shape[0], place0.shape[1]), F32)
    for grad, mask, place in (
        (feature_grad, mask_n_ref, place0),
        (encoder_ref[...], mask_w_ref, place1),
        (attention_ref[...], mask_w_ref, place2),
        (final_ref[...], mask_w_ref, place3),
    ):
        gains += jnp.dot((grad * mask[...]).astype(BF16), place[...], preferred_element_type=F32)
    streams, seqs, _, width = packed_ref.shape
    conv_rows = conv_grad.shape[0] // (streams * seqs)
    rows = projection_grad.shape[0] // (streams * seqs)
    first = lax.broadcasted_iota(jnp.int32, (8, gains.shape[1]), 0) == 0
    blank = jnp.zeros((8, width - gains.shape[1]), F32)
    for s in range(seqs):
        for f in range(streams):
            d = s * streams + f
            piece = projection_grad[d * rows : (d + 1) * rows]
            rest = piece[:, width:]
            folded = jnp.concatenate([rest[: rows // 2], rest[rows // 2 :]], axis=1)
            row = jnp.concatenate([jnp.where(first, gains[d : d + 1], 0.0), blank], axis=1)
            block = jnp.concatenate(
                [conv_grad[d * conv_rows : (d + 1) * conv_rows], piece[:, :width], folded, row],
                axis=0,
            )
            packed_ref[f ^ stream, s] = block.astype(BF16)


def front_back(
    stream, back, joined, normed, projection, before, feature_gain, unfolded, conv, gain_grads,
    streams, seqs,
):
    devices = streams * seqs
    narrow, wide = projection.shape
    counts = [narrow // devices] + [wide // devices] * 3
    masks, places, start = [], [], 0
    for size, count in zip((narrow, wide, wide, wide), counts):
        column = np.arange(size)
        masks.append((column[None] // count == np.arange(devices)[:, None]).astype(np.float32))
        place = column[:, None] % count + start == np.arange(128)[None]
        places.append(jnp.asarray(place, BF16))
        start += count
    depth = (conv.shape[0] + narrow + narrow // 2) // devices + 8
    vmem = pl.BlockSpec(memory_space=pltpu.VMEM)
    return pl.pallas_call(
        front_kernel,
        in_specs=[pl.BlockSpec(memory_space=pltpu.SMEM)] + [vmem] * 17,
        out_specs=[vmem] * 2,
        out_shape=[
            jax.ShapeDtypeStruct((streams, seqs, depth, narrow), BF16),
            jax.ShapeDtypeStruct(unfolded.shape, F32),
        ],
        compiler_params=pltpu.CompilerParams(vmem_limit_bytes=VMEM),
        cost_estimate=pl.CostEstimate(flops=0, bytes_accessed=0, transcendentals=0),
        name="front_back",
    )(
        stream, back, joined, normed, projection, before, feature_gain, unfolded, conv,
        *gain_grads, masks[0], masks[1], *places,
    )


def body(
    features,
    lengths,
    conv_weight,
    feature_gain,
    projection_weight,
    position_weight,
    encoder_gain,
    qkv_weight,
    output_weight,
    attention_gain,
    up_weight,
    down_weight,
    final_gain,
    cotangent,
):
    frames = cotangent.shape[2]
    rows = MICROS * frames
    seqs = lax.axis_size("seq")
    streams = lax.axis_size("fsdp")
    devices = seqs * streams
    me = lax.axis_index("seq")
    stream = lax.axis_index("fsdp")
    both = ("seq", "fsdp")
    group = HEAD_PARTS * MICROS
    outer = seqs // group
    near = [[o * group + i for i in range(group)] for o in range(outer)]
    far = [[o * group + i for o in range(outer)] for i in range(group)]

    def near_swap(blocks):
        return lax.all_to_all(blocks, "seq", 0, 0, axis_index_groups=near)

    def seq_sum(blocks):
        shape = (outer, group, -1, blocks.shape[-1])
        blocks = near_swap(blocks.reshape(shape).transpose(1, 0, 2, 3))
        total = jnp.sum(blocks.astype(F32), axis=0)
        if outer == 1:
            return total[0]
        return lax.psum_scatter(total, "seq", scatter_dimension=0, axis_index_groups=far)

    def near_gather(block, again):
        blocks = [block]
        for k in range(1, group):
            pairs = [(i, i - i % group + (i % group ^ k)) for i in range(seqs)]
            blocks.append(lax.ppermute(block if k < 5 else again, "seq", pairs))
        return jnp.stack(flip(blocks, me % group))

    front_rows = (conv_weight.shape[0], projection_weight.size // C_CNN)
    gains = jnp.concatenate([feature_gain, encoder_gain, attention_gain, final_gain])
    front = jnp.concatenate(
        [
            conv_weight,
            projection_weight.reshape(-1, C_CNN),
            jnp.pad(gains[None], ((0, 7), (0, C_CNN - gains.size))),
        ],
        axis=0,
    )
    part = D // HEAD_PARTS
    up_rows = up_weight.shape[0]
    unit_rows = down_weight.shape[0]
    wide = seqs * unit_rows
    up_parts = up_weight.reshape(up_rows, seqs, streams, unit_rows).transpose(2, 0, 1, 3)
    qkv_parts = qkv_weight.reshape(up_rows, 3, streams, part).transpose(2, 0, 1, 3)
    parts = jnp.concatenate(
        [qkv_parts.reshape(streams, up_rows, 3 * part), up_parts.reshape(streams, up_rows, wide)],
        axis=2,
    )
    parts = jnp.concatenate(swap_parts([parts[j] for j in range(streams)], stream), axis=0)
    front_again, parts = lax.optimization_barrier((front, parts))
    front_near = near_gather(front, front_again)
    front = front_near
    if outer > 1:
        front = lax.all_gather(front, "seq", axis=0, tiled=True, axis_index_groups=far)
    front = jnp.stack(flip(gather_blocks(front), stream), axis=1)
    front = front.reshape(devices, -1, C_CNN)
    cut = front_rows[0] + front_rows[1]
    conv_full = front[:, : front_rows[0]].reshape(-1, C_CNN)
    projection_full = front[:, front_rows[0] : cut].reshape(C_CNN, D)
    gains_full = front[:, cut, : gains.size]
    feature_n, model_n = feature_gain.size, encoder_gain.size
    feature_scale = gains_full[:, :feature_n].reshape(-1).astype(F32)
    encoder_scale, attention_scale, final_scale = (
        gains_full[:, feature_n + i * model_n : feature_n + (i + 1) * model_n]
        .reshape(-1)
        .astype(F32)
        for i in range(3)
    )

    share = D // group
    own_rows = position_weight.shape[0]
    taps = near_swap(after(position_weight, front_near).T.reshape(group, share, own_rows))

    out_parts = output_weight.reshape(up_rows, streams, part).transpose(1, 0, 2)
    quarter = jnp.concatenate(
        [parts[:, : 3 * part], out_parts.reshape(-1, part), parts[:, 3 * part :], down_weight],
        axis=1,
    )
    quarter = lax.all_gather(quarter, "seq", axis=0, tiled=True)

    ends = jnp.cumsum(lengths[:, 0], axis=-1, dtype=jnp.int32)
    positions = me * frames + jnp.arange(frames + 1, dtype=jnp.int32)
    segments = segment_of(ends, positions)
    same_next = (segments[:, 1:] == segments[:, :-1])[:, :, None]
    pairs = features[:, 0].reshape(MICROS, frames, 2 * C_CNN)
    next_first = shifted(pairs[:, :1, :C_CNN], "seq", -1)
    following = jnp.concatenate([pairs[:, 1:, :C_CNN], next_first], axis=1)
    following = following * same_next.astype(BF16)
    unfolded = jnp.concatenate([pairs, following], axis=2).reshape(rows, 3 * C_CNN)
    before = plain_dot(unfolded, conv_full)
    normed_low = norm_rows(smooth_gate(before), feature_scale).astype(BF16)
    projected = plain_dot(normed_low, projection_full)

    if outer > 1:
        taps = lax.all_gather(taps, "seq", axis=0, axis_index_groups=far)
    taps = after(taps.reshape(outer, group, share, own_rows), projected)
    position_full = (
        jnp.stack(flip([taps] + [swapped(taps, k) for k in range(1, 4)], stream))
        .transpose(3, 1, 2, 0, 4)
        .reshape(share, COARSE, FINE * CG)
        .transpose(1, 0, 2)
    )

    def to_groups(block):
        across = near_swap(block.reshape(group, share, rows))
        if outer == 1:
            return across, jnp.zeros((share, MICROS * POS_K), BF16)
        first = across[0].reshape(share, MICROS, frames)[:, :, :HALF]
        last = across[-1].reshape(share, MICROS, frames)[:, :, frames - HALF :]
        edge = [shifted(first, "seq", -group), shifted(last, "seq", group)]
        return across, jnp.concatenate(edge, axis=2).reshape(share, MICROS * POS_K)

    window, window_edge = to_groups(projected.astype(BF16).T)
    position = position_conv(window, window_edge, position_full)
    position, quarter = lax.optimization_barrier((position, quarter))
    middle = gather_blocks(quarter[:, : 4 * part])
    position = near_swap(position).reshape(D, rows)
    feed, position = lax.optimization_barrier((quarter[:, 4 * part :], position))
    feed = gather_blocks(feed)
    position_act = smooth_gate(position.T.astype(F32))
    encoded = norm_rows(projected + position_act, encoder_scale)
    encoded_low = encoded.astype(BF16)

    mixed_heads = head_projection(encoded_low, middle, 3 * part)
    mixed_heads = near_swap(mixed_heads)
    mixed_heads = mixed_heads.reshape(group, 3, part, frames)
    micro_ends = lax.dynamic_index_in_dim(ends, me % MICROS, 0, keepdims=False)
    seg_all = segment_of(micro_ends, jnp.arange(seqs * frames, dtype=jnp.int32))
    seg_own = lax.dynamic_slice_in_dim(
        seg_all, (me // group) * group * frames, group * frames, 0
    )
    output_full = jnp.stack(flip([block[:, 3 * part :] for block in middle], stream))
    output_full = (
        output_full.reshape(streams, seqs, streams, up_rows, part)
        .transpose(1, 0, 3, 2, 4)
        .reshape(HEAD_PARTS, part, D)
    )
    output_full = jnp.concatenate(flip([output_full[j] for j in range(HEAD_PARTS)], stream))
    mixed_heads, output_full = lax.optimization_barrier((mixed_heads, output_full))
    if outer > 1:
        mixed_all = lax.all_gather(
            mixed_heads, "seq", axis=0, tiled=True, axis_index_groups=far
        )
    else:
        mixed_all = mixed_heads
    context_heads = attention(mixed_heads, mixed_all, seg_own, seg_all)
    context_low = near_swap(context_heads.astype(BF16))

    (
        block_out, mid_grad, context_grad, attention_grad, final_grad,
        settled_low, hidden_low, fed_low, up_low, branch_low,
    ) = feed_forward(
        context_low, output_full, encoded, attention_scale[None], final_scale[None],
        cotangent[:, 0].reshape(rows, D), feed,
    )
    context_grad = near_swap(context_grad)
    feed_grads = feed_grad(stream[None], settled_low, up_low, hidden_low, fed_low, seqs)
    context_grad, feed_grads = lax.optimization_barrier((context_grad, feed_grads))
    feed_grads = feed_grads.reshape(devices, -1, D)
    feed_shard = lax.psum_scatter(feed_grads, both, scatter_dimension=0)
    context_low = context_low.reshape(HEAD_PARTS, MICROS, part, frames).transpose(0, 2, 1, 3)
    output_grad = plain_dot(context_low.reshape(D, rows), branch_low).astype(BF16)
    output_grad = output_grad.reshape(HEAD_PARTS, part, D)
    output_grad = jnp.stack(flip([output_grad[j] for j in range(HEAD_PARTS)], stream))
    output_grad = (
        output_grad.reshape(seqs, streams, up_rows, streams, part)
        .transpose(1, 0, 3, 2, 4)
        .reshape(streams, D, part)
    )
    output_grads = flip([output_grad[j] for j in range(streams)], stream)

    dq, dk, dv = attention_back(
        mixed_heads, mixed_all, context_grad, context_heads, seg_own, seg_all
    )
    if outer > 1:
        dk, dv = (
            lax.psum_scatter(
                grad, "seq", scatter_dimension=0, tiled=True, axis_index_groups=far
            )
            for grad in (dk, dv)
        )
    mixed_g = near_swap(jnp.stack([dq, dk, dv], axis=1)).reshape(group, 3 * part, frames)
    joined_grad, position_grad, encoder_grad = head_back(
        mixed_g, mid_grad, position, projected, encoder_scale[None], middle, 3 * part
    )
    mixed_g = mixed_g.reshape(HEAD_PARTS, MICROS, 3 * part, frames).transpose(0, 2, 1, 3)
    mixed_g = mixed_g.reshape(HEAD_PARTS, 3 * part, rows)
    middle_grads = [
        jnp.concatenate(
            [
                lax.dot_general(
                    encoded_low, mixed_g[k], (((0,), (1,)), ((), ())), preferred_element_type=F32
                ).astype(BF16),
                output_grads[k],
            ],
            axis=1,
        )
        for k in range(HEAD_PARTS)
    ]

    grad_window, grad_edge = to_groups(position_grad)
    grad_window, middle_pairs = lax.optimization_barrier((grad_window, pair_sums(middle_grads)))
    middle_sum = low_sum(middle_pairs[0], swapped(middle_pairs[1], 2))
    projected_back, taps_grad = position_back(
        window, window_edge, grad_window, grad_edge, position_full
    )


    projected_back = near_swap(projected_back).reshape(D, rows)
    projected_back, middle_sum = lax.optimization_barrier((projected_back, middle_sum))
    front_grads, unfolded_grad = front_back(
        stream[None], projected_back, joined_grad, normed_low, projection_full, before,
        feature_scale[None], unfolded, conv_full, (encoder_grad, attention_grad, final_grad),
        streams, seqs,
    )
    unfolded_grad = unfolded_grad.reshape(MICROS, frames, 3 * C_CNN)
    middle_shard = seq_sum(after(middle_sum, front_grads))
    following_grad = unfolded_grad[:, :, 2 * C_CNN :] * same_next.astype(F32)
    carried = shifted(following_grad[:, frames - 1 :], "seq", 1)
    even_grad = unfolded_grad[:, :, :C_CNN] + jnp.concatenate(
        [carried, following_grad[:, :-1]], axis=1
    )
    input_grad = jnp.concatenate([even_grad, unfolded_grad[:, :, C_CNN : 2 * C_CNN]], axis=2)
    input_grad = input_grad.reshape(MICROS, 1, 2 * frames, C_CNN)

    front_pairs = pair_sums([front_grads[k] for k in range(streams)])
    taps_grad = after(taps_grad, front_pairs[1])
    front_sum = low_sum(front_pairs[0], swapped(front_pairs[1], 2))
    front_shard = seq_sum(front_sum)
    front_shard, middle_shard = lax.optimization_barrier((front_shard, middle_shard))

    taps_grad = (
        taps_grad.transpose(1, 0, 2)
        .reshape(share, outer, group, streams, own_rows)
        .transpose(3, 1, 2, 0, 4)
    )
    taps_grad = reduce_blocks(flip([taps_grad[j] for j in range(streams)], stream))
    taps_grad = after(taps_grad, front_sum)
    if outer > 1:
        taps_grad = lax.psum_scatter(
            taps_grad, "seq", scatter_dimension=0, axis_index_groups=far
        )
    else:
        taps_grad = taps_grad[0]
    position_shard = near_swap(taps_grad).reshape(D, own_rows).T.astype(F32)

    def unswap(block):
        block = block.reshape(streams, up_rows, -1)
        return jnp.stack(swap_parts([block[j] for j in range(streams)], stream)).astype(F32)

    feed_shard = feed_shard.reshape(2, streams, up_rows, wide).astype(F32)
    down_shard = feed_shard[0].reshape(unit_rows, D)
    up_shard = (
        feed_shard[1]
        .reshape(streams, up_rows, seqs, unit_rows)
        .transpose(1, 2, 0, 3)
        .reshape(up_rows, -1)
    )
    qkv_shard = (
        unswap(middle_shard[:, : 3 * part])
        .reshape(streams, up_rows, 3, part)
        .transpose(1, 2, 0, 3)
        .reshape(up_rows, -1)
    )
    output_shard = (
        middle_shard[:, 3 * part :]
        .reshape(streams, up_rows, part)
        .transpose(1, 0, 2)
        .reshape(up_rows, D)
        .astype(F32)
    )
    conv_rows, projection_rows = conv_weight.shape[0], projection_weight.shape[0]
    conv_shard = front_shard[:conv_rows]
    cut = conv_rows + projection_rows
    folded = front_shard[cut : cut + projection_rows // 2]
    folded = jnp.concatenate([folded[:, : D - C_CNN], folded[:, D - C_CNN :]], axis=0)
    projection_shard = jnp.concatenate([front_shard[conv_rows:cut], folded], axis=1)
    gain_row = front_shard[cut + projection_rows // 2]
    gain_shards = [
        gain_row[:feature_n],
        *(gain_row[feature_n + i * model_n : feature_n + (i + 1) * model_n] for i in range(3)),
    ]
    return (
        block_out.reshape(MICROS, 1, frames, D),
        input_grad,
        conv_shard,
        gain_shards[0],
        projection_shard,
        position_shard,
        gain_shards[1],
        qkv_shard,
        output_shard,
        gain_shards[2],
        up_shard,
        down_shard,
        gain_shards[3],
    )


def solution(mesh):
    weight, gain = P(("seq", "fsdp"), None), P(("seq", "fsdp"))
    rows = P(None, "fsdp", "seq", None)
    in_specs = (
        rows, P(None, "fsdp", None), weight, gain, weight, weight, gain, weight, weight, gain,
        weight, weight, gain, rows,
    )
    out_specs = (
        rows, rows, weight, gain, weight, weight, gain, weight, weight, gain, weight, weight, gain,
    )
    return jax.shard_map(body, mesh=mesh, in_specs=in_specs, out_specs=out_specs, check_vma=False)
```

profile of v0, /device:TPU:0, one launch (start us, length us, event | category | flops | bytes accessed | tf_op | source)
XLA Modules:
  0.0 519.7 jit_solution(3013107390876687922)
XLA Ops:
  10.7 2.6 collective-permute-start.7
  13.5 2.1 collective-permute-start.1
  15.6 1.6 collective-permute-start.2
  17.1 3.0 collective-permute-start.4
  20.2 2.4 collective-permute-start.10
  22.6 1.6 collective-permute-start.8
  26.5 2.0 collective-permute-done.10
  28.5 6.6 %collective-permute-done.8 = bf16[80,512]{1,0:T(8,128)(2,1)S(1)} collective-permute-done((bf16[80,512]{1,0:T(8,128)(2,1)S(1)}, bf16[80,512]{1,0:T(8,128)(2,1)S(1)}, u32[]{:S(2)}, u32[]{:S(2)}) %collective-permute-start.8) | collective-permute-done | bytes 81952 | tf_op jit(solution)/shard_map/ppermute | solution.py:709
  39.6 11.6 %collective-permute-done.12 = bf16[8,80,512]{2,1,0:T(8,128)(2,1)} collective-permute-done((bf16[8,80,512]{2,1,0:T(8,128)(2,1)S(1)}, bf16[8,80,512]{2,1,0:T(8,128)(2,1)}, u32[]{:S(2)}, u32[]{:S(2)}) %collective-permute-start.12) | collective-permute-done | bytes 655392 | tf_op jit(solution)/shard_map/ppermute | solution.py:44
  52.6 4.7 all-to-all-start.1
  57.3 2.1 select_bitcast_fusion.3
  59.9 2.1 fusion.71
  64.3 15.6 %all-to-all-done.1 = bf16[8,96,192]{2,1,0:T(8,128)(2,1)S(1)} async-done(((bf16[8,96,192]{2,1,0:T(8,128)(2,1)}), bf16[8,96,192]{2,1,0:T(8,128)(2,1)S(1)}, u32[]{:S(2)}, u32[]{:S(2)}) %all-to-all-start.1) | async-done | bytes 294944 | tf_op jit(solution)/shard_map/all_to_all | solution.py:695
  82.7 4.7 all-to-all-start
  87.5 4.3 collective-permute-done.15
  92.5 7.0 %collective-permute-done.16 = bf16[1,8,96,192]{3,2,1,0:T(8,128)(2,1)} collective-permute-done((bf16[1,8,96,192]{3,2,1,0:T(8,128)(2,1)S(1)}, bf16[1,8,96,192]{3,2,1,0:T(8,128)(2,1)}, u32[]{:S(2)}, u32[]{:S(2)}) %collective-permute-start.16) | collective-permute-done | bytes 294944 | tf_op jit(solution)/shard_map/ppermute | solution.py:44
  102.5 2.3 reshape.596
  104.7 1.7 all-to-all-done.refs_0_
  107.2 6.2 %position_conv.1 = bf16[8,96,256]{2,1,0:T(8,128)(2,1)} custom-call(bf16[8,96,256]{2,1,0:T(8,128)(2,1)} %copy-done.11, bf16[96,256]{1,0:T(8,128)(2,1)} %broadcast_7_refs_1__refs_3_.2.refs_1_.refs_3_, bf16[8,96,768]{2,1,0:T(8,128)(2,1)} %bitcast.335), custom_call_target="tpu_custom_call" | custom-call | tf_op jit(solution)/shard_map/position_conv/pallas_call | solution.py:189
  113.4 3.5 all-to-all-start.2
  119.8 3.3 slice.263.feed0
  123.1 5.8 %all-to-all-done.2 = bf16[8,96,256]{2,1,0:T(8,128)(2,1)S(1)} async-done(((bf16[8,96,256]{2,1,0:T(8,128)(2,1)}), bf16[8,96,256]{2,1,0:T(8,128)(2,1)S(1)}, u32[]{:S(2)}, u32[]{:S(2)}) %all-to-all-start.2) | async-done | bytes 393248 | tf_op jit(solution)/shard_map/all_to_all | solution.py:695
  132.4 14.8 %collective-permute-done.18.refs_3_.refs_7_ = bf16[768,768]{1,0:T(8,128)(2,1)S(1)} collective-permute-done((bf16[768,768]{1,0:T(8,128)(2,1)S(1)}, bf16[768,768]{1,0:T(8,128)(2,1)S(1)}, u32[]{:S(2)}, u32[]{:S(2)}) %collective-permute-start.18) | collective-permute-done | bytes 1179680 | tf_op jit(solution)/shard_map/ppermute | solution.py:44
  147.2 3.3 fusion.69
  152.7 5.0 head_projection.1
  157.6 6.3 %all-to-all-start.3 = ((bf16[8,576,128]{2,1,0:T(8,128)(2,1)}), bf16[8,576,128]{2,1,0:T(8,128)(2,1)S(1)}, u32[]{:S(2)}, u32[]{:S(2)}) async-start(bf16[8,576,128]{2,1,0:T(8,128)(2,1)} %head_projection.1), calls=%async_computation.3 | async-start | bytes 2359296 | tf_op jit(solution)/shard_map/all_to_all | solution.py:695
  164.0 32.8 %collective-permute-done.21.feed2 = bf16[768,1536]{1,0:T(8,128)(2,1)} collective-permute-done((bf16[768,1536]{1,0:T(8,128)(2,1)}, bf16[768,1536]{1,0:T(8,128)(2,1)}, u32[]{:S(2)}, u32[]{:S(2)}) %collective-permute-start.21) | collective-permute-done | bytes 2359328 | tf_op jit(solution)/shard_map/ppermute | solution.py:44
  198.0 2.0 select_select_fusion.11
  206.8 6.5 %attention.1.refs_4_ = f32[8,192,128]{2,1,0:T(8,128)} custom-call(bf16[8,3,192,128]{3,2,1,0:T(8,128)(2,1)} %bitcast.323, bf16[8,3,192,128]{3,2,1,0:T(8,128)(2,1)} %bitcast.324, bf16[8,3,192,128]{3,2,1,0:T(8,128)(2,1)} %bitcast.325, s32[1024,1]{1,0:T(8,128)} %copy.226.refs_3_.refs_6_, s32[1,1024]{1,0:T(1,128)} %bitcast.384), custom_call_target="tpu_custom_call" | custom-call | tf_op jit(solution)/shard_map/attention/pallas_call | solution.py:320
  213.3 2.0 convert_element_type.252
  215.4 6.1 %all-to-all-start.4 = ((bf16[8,192,128]{2,1,0:T(8,128)(2,1)}), bf16[8,192,128]{2,1,0:T(8,128)(2,1)S(1)}, u32[]{:S(2)}, u32[]{:S(2)}) async-start(bf16[8,192,128]{2,1,0:T(8,128)(2,1)} %convert_element_type.252), calls=%async_computation.4 | async-start | bytes 786432 | tf_op jit(solution)/shard_map/all_to_all | solution.py:695
  224.0 9.8 %all-to-all-done.4.ctx_ref = bf16[8,192,128]{2,1,0:T(8,128)(2,1)S(1)} async-done(((bf16[8,192,128]{2,1,0:T(8,128)(2,1)}), bf16[8,192,128]{2,1,0:T(8,128)(2,1)S(1)}, u32[]{:S(2)}, u32[]{:S(2)}) %all-to-all-start.4) | async-done | bytes 393248 | tf_op jit(solution)/shard_map/all_to_all | solution.py:695
  234.6 12.6 %feed_forward.1 = (f32[256,768]{1,0:T(8,128)}, f32[256,768]{1,0:T(8,128)}, bf16[8,192,128]{2,1,0:T(8,128)(2,1)}, f32[1,768]{1,0:T(1,128)}, f32[1,768]{1,0:T(1,12...) custom-call(bf16[8,192,128]{2,1,0:T(8,128)(2,1)} %copy-done.9, ...), custom_call_target="tpu_custom_call" | custom-call | tf_op jit(solution)/shard_map/feed_forward/pallas_call | solution.py:469
  247.2 3.9 all-to-all-start.5
  251.1 8.5 %feed_grad.1 = bf16[8,4,2,4,24,768]{5,4,3,2,1,0:T(8,128)(2,1)} custom-call(s32[1]{0:T(128)} %bitcast.55.stream_ref, bf16[256,768]{1,0:T(8,128)(2,1)} %get-tuple-element.67.settled_ref, bf16[256,3072]{1,0:T(8,128)(2,1)} %get-tuple-element.68.up_ref, bf16[256,3072]{1,0:T(8,128)(2,1)} %get-tuple-element.69.hidden_ref, bf16[256,768]{1,0:T(8,128)(2,1)} %get-tuple-element.70.fed_ref), custom_call_target="tpu_custom_call" | custom-call | tf_op jit(solution)/shard_map/feed_grad/pallas_call | solution.py:520
  259.6 3.3 all-to-all-done.5.refs_3_
  263.7 15.5 %attention_back.1 = (bf16[8,192,128]{2,1,0:T(8,128)(2,1)}, bf16[8,192,128]{2,1,0:T(8,128)(2,1)}, bf16[8,192,128]{2,1,0:T(8,128)(2,1)}) custom-call(bf16[8,3,192,128]{3,2,1,0:T(8,128)(2,1)} %bitcast.326, bf16[8,3,192,128]{3,2,1,0:T(8,128)(2,1)} %bitcast.327, bf16[8,3,192,128]{3,2,1,0:T(8,128)(2,1)} %bitcast.328, bf16[8,192,128]{2,1,0:T(8,128)(2,1)} %copy-done.19, ...), custom_call_target="tpu_custom_call" | custom-call | tf_op jit(solution)/shard_map/attention_back/pallas_call | solution.py:344
  281.7 3.8 all-to-all-start.6
  287.0 2.3 reshape.606
  289.3 1.7 copy.281
  292.2 1.9 copy.239
  295.2 19.0 %all-to-all-done.6 = bf16[8,3,192,128]{3,2,1,0:T(8,128)(2,1)S(1)} async-done(((bf16[8,3,192,128]{3,2,1,0:T(8,128)(2,1)}), bf16[8,3,192,128]{3,2,1,0:T(8,128)(2,1)S(1)}, u32[]{:S(2)}, u32[]{:S(2)}) %all-to-all-start.6) | async-done | bytes 1179680 | tf_op jit(solution)/shard_map/all_to_all | solution.py:695
  320.6 6.5 %head_back.1 = (f32[256,768]{1,0:T(8,128)}, bf16[768,256]{1,0:T(8,128)(2,1)}, f32[1,768]{1,0:T(1,128)}) custom-call(bf16[8,576,128]{2,1,0:T(8,128)(2,1)} %bitcast.334, f32[256,768]{1,0:T(8,128)} %get-tuple-element.75.refs_1_, bf16[768,256]{1,0:T(8,128)(2,1)} %bitcast.345, f32[256,768]{1,0:T(8,128)} %copy-done.1, f32[1,768]{1,0:T(1,128)} %reshape.621.refs_4_, ...), custom_call_target="tpu_custom_call" | custom-call | tf_op jit(solution)/shard_map/head_back/pallas_call | solution.py:575
  327.1 3.9 all-to-all-start.7
  331.9 2.6 add_convert_fusion.1
  334.6 1.7 add_convert_fusion.2
  336.3 6.6 %all-to-all-done.7.refs_2_ = bf16[8,96,256]{2,1,0:T(8,128)(2,1)S(1)} async-done(((bf16[8,96,256]{2,1,0:T(8,128)(2,1)}), bf16[8,96,256]{2,1,0:T(8,128)(2,1)S(1)}, u32[]{:S(2)}, u32[]{:S(2)}) %all-to-all-start.7) | async-done | bytes 393248 | tf_op jit(solution)/shard_map/all_to_all | solution.py:695
  344.3 12.1 %position_back.1 = (bf16[8,96,256]{2,1,0:T(8,128)(2,1)}, bf16[8,96,768]{2,1,0:T(8,128)(2,1)}) custom-call(bf16[8,96,256]{2,1,0:T(8,128)(2,1)} %copy-done.11, bf16[96,256]{1,0:T(8,128)(2,1)} %broadcast_7_refs_1__refs_3_.2.refs_1_.refs_3_, bf16[8,96,256]{2,1,0:T(8,128)(2,1)} %copy-done.20, bf16[96,256]{1,0:T(8,128)(2,1)} %broadcast_7_refs_1__refs_3_.2.refs_1_.refs_3_, ...), custom_call_target="tpu_custom_call" | custom-call | tf_op jit(solution)/shard_map/position_back/pallas_call | solution.py:208
  356.4 4.1 all-to-all-start.8
  362.1 14.7 %collective-permute-done.25 = bf16[768,768]{0,1:T(8,128)(2,1)} collective-permute-done((bf16[768,768]{0,1:T(8,128)(2,1)}, bf16[768,768]{0,1:T(8,128)(2,1)}, u32[]{:S(2)}, u32[]{:S(2)}) %collective-permute-start.25) | collective-permute-done | bytes 1179680 | tf_op jit(solution)/shard_map/ppermute | solution.py:44
  376.8 1.6 add_convert_fusion
  378.4 4.2 all-to-all-done.8
  383.3 6.8 %front_back.1 = (bf16[4,8,80,512]{3,2,1,0:T(8,128)(2,1)}, f32[256,1536]{1,0:T(8,128)}) custom-call(s32[1]{0:T(128)} %bitcast.55.stream_ref, bf16[768,256]{1,0:T(8,128)(2,1)} %bitcast.360, f32[256,768]{1,0:T(8,128)} %get-tuple-element.83.joined_ref, bf16[256,512]{1,0:T(8,128)(2,1)} %copy-done.13, bf16[512,768]{1,0:T(8,128)(2,1)} %copy-done.4, ...), custom_call_target="tpu_custom_call" | custom-call | tf_op jit(solution)/shard_map/front_back/pallas_call | solution.py:648
  391.6 2.1 collective-permute-done.28
  393.7 2.1 fusion
  395.8 3.5 reshape.610
  403.3 26.9 %collective-permute-done.32 = bf16[1,8,96,192]{3,2,1,0:T(8,128)(2,1)S(1)} collective-permute-done((bf16[1,8,96,192]{3,2,1,0:T(8,128)(2,1)S(1)}, bf16[1,8,96,192]{3,2,1,0:T(8,128)(2,1)S(1)}, u32[]{:S(2)}, u32[]{:S(2)}) %collective-permute-start.32) | collective-permute-done | bytes 294944 | tf_op jit(solution)/shard_map/ppermute | solution.py:44
  431.4 2.2 add_convert_fusion.3
  433.6 3.5 all-to-all-start.11
  437.7 11.2 %all-to-all-done.11 = bf16[8,96,192]{2,1,0:T(8,128)(2,1)S(1)} async-done(((bf16[8,96,192]{2,1,0:T(8,128)(2,1)}), bf16[8,96,192]{2,1,0:T(8,128)(2,1)S(1)}, u32[]{:S(2)}, u32[]{:S(2)}) %all-to-all-start.11) | async-done | bytes 294944 | tf_op jit(solution)/shard_map/all_to_all | solution.py:695
  448.9 32.6 %all_to_all.60 = bf16[8,1,96,768]{3,2,1,0:T(8,128)(2,1)S(1)} all-to-all(bf16[8,1,96,768]{3,2,1,0:T(8,128)(2,1)S(1)} %bitcast.343), channel_id=1, replica_groups={{0,4,8,12,16,20,24,28},{1,5,9,13,17,21,25,29},{2,6,10,14,18,22,26,30},{..., dimensions={0} | all-to-all | bytes 2359296 | tf_op jit(solution)/shard_map/all_to_all | solution.py:695
  481.5 3.5 all-to-all-start.9
  486.2 3.8 collective-permute-start.26
  495.2 6.6 %all-to-all-done.9 = bf16[8,1,80,512]{3,2,1,0:T(8,128)(2,1)S(1)} async-done(((bf16[8,1,80,512]{3,2,1,0:T(8,128)(2,1)}), bf16[8,1,80,512]{3,2,1,0:T(8,128)(2,1)S(1)}, u32[]{:S(2)}, u32[]{:S(2)}) %all-to-all-start.9) | async-done | bytes 655392 | tf_op jit(solution)/shard_map/all_to_all | solution.py:695
  (303 shorter events, 82.8 us)
Async XLA Ops:
  7.2 106.2 %all-gather.2.cloned.1.call-start = ((), (), s32[]{:S(2)}) async-start(), calls=%async_computation.13 | async-start | bytes 3981312 | tf_op jit(solution)/shard_map/all_gather | solution.py:762
  9.8 15.5 %copy-start.39 = (bf16[24,768]{1,0:T(8,128)(2,1)S(1)}, bf16[24,768]{1,0:T(8,128)(2,1)}, u32[]{:S(2)}) copy-start(bf16[24,768]{1,0:T(8,128)(2,1)} %param.28) | copy-start | bytes 110596
  10.1 15.5 %copy-start.31 = (bf16[96,768]{1,0:T(8,128)(2,1)S(1)}, bf16[96,768]{1,0:T(8,128)(2,1)}, u32[]{:S(2)}) copy-start(bf16[96,768]{1,0:T(8,128)(2,1)} %param.31) | copy-start | bytes 442372
  10.1 7.0 %collective-permute-start.5 = (bf16[24,1344]{1,0:T(8,128)(2,1)S(1)}, bf16[24,1344]{1,0:T(8,128)(2,1)S(1)}, u32[]{:S(2)}, u32[]{:S(2)}) collective-permute-start(bf16[24,1344]{1,0:T(8,128)(2,1)S(1)} %get-tuple-element.233), channel_id=1, source_target_pairs={{0,1},{1,0},{2,3},{3,2},{4,5},{5,4},{6,7},{7,6},{8,9},{9,8},{10,11... | collective-permute-start | bytes 193544 | tf_op jit(solution)/shard_map/ppermute | solution.py:44
  10.7 6.5 %collective-permute-start.7 = (bf16[24,1344]{1,0:T(8,128)(2,1)S(1)}, bf16[24,1344]{1,0:T(8,128)(2,1)S(1)}, u32[]{:S(2)}, u32[]{:S(2)}) collective-permute-start(bf16[24,1344]{1,0:T(8,128)(2,1)S(1)} %get-tuple-element.232), channel_id=1, source_target_pairs={{0,3},{1,2},{2,1},{3,0},{4,7},{5,6},{6,5},{7,4},{8,11},{9,10},{10,... | collective-permute-start | bytes 193544 | tf_op jit(solution)/shard_map/ppermute | solution.py:44
  13.3 6.9 %collective-permute-start.6 = (bf16[24,1344]{1,0:T(8,128)(2,1)S(1)}, bf16[24,1344]{1,0:T(8,128)(2,1)S(1)}, u32[]{:S(2)}, u32[]{:S(2)}) collective-permute-start(bf16[24,1344]{1,0:T(8,128)(2,1)S(1)} %get-tuple-element.187), channel_id=1, source_target_pairs={{0,2},{1,3},{2,0},{3,1},{4,6},{5,7},{6,4},{7,5},{8,10},{9,11},{10,... | collective-permute-start | bytes 193544 | tf_op jit(solution)/shard_map/ppermute | solution.py:44
  13.5 9.1 %collective-permute-start.1 = (bf16[80,512]{1,0:T(8,128)(2,1)S(1)}, bf16[80,512]{1,0:T(8,128)(2,1)S(1)}, u32[]{:S(2)}, u32[]{:S(2)}) collective-permute-start(bf16[80,512]{1,0:T(8,128)(2,1)S(1)} %fusion.57), channel_id=1, source_target_pairs={{0,4},{4,0},{8,12},{12,8},{16,20},{20,16},{24,28},{28,24},{1,5},{5... | collective-permute-start | bytes 245768 | tf_op jit(solution)/shard_map/ppermute | solution.py:709
  15.6 8.7 %collective-permute-start.2 = (bf16[80,512]{1,0:T(8,128)(2,1)S(1)}, bf16[80,512]{1,0:T(8,128)(2,1)S(1)}, u32[]{:S(2)}, u32[]{:S(2)}) collective-permute-start(bf16[80,512]{1,0:T(8,128)(2,1)S(1)} %fusion.57), channel_id=1, source_target_pairs={{0,8},{4,12},{8,0},{12,4},{16,24},{20,28},{24,16},{28,20},{1,9},{5... | collective-permute-start | bytes 245768 | tf_op jit(solution)/shard_map/ppermute | solution.py:709
  17.1 9.3 %collective-permute-start.3 = (bf16[80,512]{1,0:T(8,128)(2,1)S(1)}, bf16[80,512]{1,0:T(8,128)(2,1)S(1)}, u32[]{:S(2)}, u32[]{:S(2)}) collective-permute-start(bf16[80,512]{1,0:T(8,128)(2,1)S(1)} %fusion.57), channel_id=1, source_target_pairs={{0,12},{4,8},{8,4},{12,0},{16,28},{20,24},{24,20},{28,16},{1,13},{... | collective-permute-start | bytes 245768 | tf_op jit(solution)/shard_map/ppermute | solution.py:709
  17.1 9.3 %collective-permute-start.4 = (bf16[80,512]{1,0:T(8,128)(2,1)S(1)}, bf16[80,512]{1,0:T(8,128)(2,1)S(1)}, u32[]{:S(2)}, u32[]{:S(2)}) collective-permute-start(bf16[80,512]{1,0:T(8,128)(2,1)S(1)} %fusion.57), channel_id=1, source_target_pairs={{0,16},{4,20},{8,24},{12,28},{16,0},{20,4},{24,8},{28,12},{1,17},{... | collective-permute-start | bytes 245768 | tf_op jit(solution)/shard_map/ppermute | solution.py:709
  20.2 8.3 %collective-permute-start.10 = (bf16[80,512]{1,0:T(8,128)(2,1)S(1)}, bf16[80,512]{1,0:T(8,128)(2,1)S(1)}, u32[]{:S(2)}, u32[]{:S(2)}) collective-permute-start(bf16[80,512]{1,0:T(8,128)(2,1)S(1)} %fusion.57), channel_id=1, source_target_pairs={{0,28},{4,24},{8,20},{12,16},{16,12},{20,8},{24,4},{28,0},{1,29},{... | collective-permute-start | bytes 245768 | tf_op jit(solution)/shard_map/ppermute | solution.py:709
  22.6 12.5 %collective-permute-start.8 = (bf16[80,512]{1,0:T(8,128)(2,1)S(1)}, bf16[80,512]{1,0:T(8,128)(2,1)S(1)}, u32[]{:S(2)}, u32[]{:S(2)}) collective-permute-start(bf16[80,512]{1,0:T(8,128)(2,1)S(1)} %fusion.57), channel_id=1, source_target_pairs={{0,20},{4,16},{8,28},{12,24},{16,4},{20,0},{24,12},{28,8},{1,21},{... | collective-permute-start | bytes 245768 | tf_op jit(solution)/shard_map/ppermute | solution.py:709
  24.3 10.8 %collective-permute-start.9 = (bf16[80,512]{1,0:T(8,128)(2,1)S(1)}, bf16[80,512]{1,0:T(8,128)(2,1)S(1)}, u32[]{:S(2)}, u32[]{:S(2)}) collective-permute-start(bf16[80,512]{1,0:T(8,128)(2,1)S(1)} %fusion.57), channel_id=1, source_target_pairs={{0,24},{4,28},{8,16},{12,20},{16,8},{20,12},{24,0},{28,4},{1,25},{... | collective-permute-start | bytes 245768 | tf_op jit(solution)/shard_map/ppermute | solution.py:709
  35.9 15.3 %collective-permute-start.12 = (bf16[8,80,512]{2,1,0:T(8,128)(2,1)S(1)}, bf16[8,80,512]{2,1,0:T(8,128)(2,1)}, u32[]{:S(2)}, u32[]{:S(2)}) collective-permute-start(bf16[8,80,512]{2,1,0:T(8,128)(2,1)S(1)} %bitcast_dynamic-update-slice_fusion), channel_id=1, source_target_pairs={{0,2},{1,3},{2,0},{3,1},{4,6},{5,7},{6,4},{7,5},{8,10},{9,11},{10,... | collective-permute-start | bytes 1966088 | tf_op jit(solution)/shard_map/ppermute | solution.py:44
  37.6 14.0 %copy-start.30 = (bf16[192,768]{1,0:T(8,128)(2,1)S(1)}, bf16[192,768]{1,0:T(8,128)(2,1)}, u32[]{:S(2)}) copy-start(bf16[192,768]{1,0:T(8,128)(2,1)} %param.25) | copy-start | bytes 884740
  37.7 13.9 %collective-permute-start = (bf16[2,1,512]{2,1,0:T(2,128)(2,1)S(1)}, bf16[2,1,512]{2,1,0:T(2,128)(2,1)S(1)}, u32[]{:S(2)}, u32[]{:S(2)}) collective-permute-start(bf16[2,1,512]{2,1,0:T(2,128)(2,1)S(1)} %slice.321), channel_id=1, source_target_pairs={{4,0},{8,4},{12,8},{16,12},{20,16},{24,20},{28,24},{5,1},{9,5},{13... | collective-permute-start | bytes 6152 | tf_op jit(solution)/shard_map/ppermute | solution.py:34
  39.5 17.8 %collective-permute-start.11 = (bf16[8,80,512]{2,1,0:T(8,128)(2,1)S(1)}, bf16[8,80,512]{2,1,0:T(8,128)(2,1)}, u32[]{:S(2)}, u32[]{:S(2)}) collective-permute-start(bf16[8,80,512]{2,1,0:T(8,128)(2,1)S(1)} %bitcast_dynamic-update-slice_fusion), channel_id=1, source_target_pairs={{0,1},{1,0},{2,3},{3,2},{4,5},{5,4},{6,7},{7,6},{8,9},{9,8},{10,11... | collective-permute-start | bytes 1966088 | tf_op jit(solution)/shard_map/ppermute | solution.py:44
  51.2 6.1 %collective-permute-start.13 = (bf16[8,80,512]{2,1,0:T(8,128)(2,1)}, bf16[8,80,512]{2,1,0:T(8,128)(2,1)}, u32[]{:S(2)}, u32[]{:S(2)}) collective-permute-start(bf16[8,80,512]{2,1,0:T(8,128)(2,1)} %collective-permute-done.12), channel_id=1, source_target_pairs={{0,1},{1,0},{2,3},{3,2},{4,5},{5,4},{6,7},{7,6},{8,9},{9,8},{10,11... | collective-permute-start | bytes 1966088 | tf_op jit(solution)/shard_map/ppermute | solution.py:44
  51.5 8.4 %copy-start.14 = (bf16[256,1024]{1,0:T(8,128)(2,1)}, bf16[256,1024]{1,0:T(8,128)(2,1)S(1)}, u32[]{:S(2)}) copy-start(bf16[256,1024]{1,0:T(8,128)(2,1)S(1)} %concatenate.55) | copy-start | bytes 1572868
  51.7 8.3 %copy-start.25 = (bf16[256,512]{1,0:T(8,128)(2,1)}, bf16[256,512]{1,0:T(8,128)(2,1)S(1)}, u32[]{:S(2)}) copy-start(bf16[256,512]{1,0:T(8,128)(2,1)S(1)} %bitcast_multiply_fusion) | copy-start | bytes 786436
  52.6 27.3 %all-to-all-start.1 = ((bf16[8,96,192]{2,1,0:T(8,128)(2,1)}), bf16[8,96,192]{2,1,0:T(8,128)(2,1)S(1)}, u32[]{:S(2)}, u32[]{:S(2)}) async-start(bf16[8,96,192]{2,1,0:T(8,128)(2,1)} %bitcast.30), calls=%async_computation.1 | async-start | bytes 786432 | tf_op jit(solution)/shard_map/all_to_all | solution.py:695
  62.9 18.9 %copy-start.4 = (bf16[512,768]{1,0:T(8,128)(2,1)}, bf16[512,768]{1,0:T(8,128)(2,1)S(1)}, u32[]{:S(2)}) copy-start(bf16[512,768]{1,0:T(8,128)(2,1)S(1)} %reshape.592.projection_ref) | copy-start | bytes 2359300
  64.3 66.1 %copy-start.1 = (f32[256,768]{1,0:T(8,128)}, f32[256,768]{1,0:T(8,128)S(1)}, u32[]{:S(2)}) copy-start(f32[256,768]{1,0:T(8,128)S(1)} %fusion.78.refs_3_) | copy-start | bytes 2359300
  79.9 7.6 %collective-permute-start.14 = (bf16[1,8,96,192]{3,2,1,0:T(8,128)(2,1)S(1)}, bf16[1,8,96,192]{3,2,1,0:T(8,128)(2,1)S(1)}, u32[]{:S(2)}, u32[]{:S(2)}) collective-permute-start(bf16[1,8,96,192]{3,2,1,0:T(8,128)(2,1)S(1)} %bitcast.354), channel_id=1, source_target_pairs={{0,1},{1,0},{2,3},{3,2},{4,5},{5,4},{6,7},{7,6},{8,9},{9,8},{10,11... | collective-permute-start | bytes 884744 | tf_op jit(solution)/shard_map/ppermute | solution.py:44
  79.9 11.9 %collective-permute-start.15 = (bf16[1,8,96,192]{3,2,1,0:T(8,128)(2,1)S(1)}, bf16[1,8,96,192]{3,2,1,0:T(8,128)(2,1)S(1)}, u32[]{:S(2)}, u32[]{:S(2)}) collective-permute-start(bf16[1,8,96,192]{3,2,1,0:T(8,128)(2,1)S(1)} %bitcast.355), channel_id=1, source_target_pairs={{0,2},{1,3},{2,0},{3,1},{4,6},{5,7},{6,4},{7,5},{8,10},{9,11},{10,... | collective-permute-start | bytes 884744 | tf_op jit(solution)/shard_map/ppermute | solution.py:44
  81.0 18.6 %collective-permute-start.16 = (bf16[1,8,96,192]{3,2,1,0:T(8,128)(2,1)S(1)}, bf16[1,8,96,192]{3,2,1,0:T(8,128)(2,1)}, u32[]{:S(2)}, u32[]{:S(2)}) collective-permute-start(bf16[1,8,96,192]{3,2,1,0:T(8,128)(2,1)S(1)} %bitcast.356), channel_id=1, source_target_pairs={{0,3},{1,2},{2,1},{3,0},{4,7},{5,6},{6,5},{7,4},{8,11},{9,10},{10,... | collective-permute-start | bytes 884744 | tf_op jit(solution)/shard_map/ppermute | solution.py:44
  82.7 23.7 %all-to-all-start = ((bf16[8,96,256]{2,1,0:T(8,128)(2,1)}), bf16[8,96,256]{2,1,0:T(8,128)(2,1)S(1)}, u32[]{:S(2)}, u32[]{:S(2)}) async-start(bf16[8,96,256]{2,1,0:T(8,128)(2,1)} %bitcast.28), calls=%async_computation | async-start | bytes 786432 | tf_op jit(solution)/shard_map/all_to_all | solution.py:695
  113.4 15.5 %all-to-all-start.2 = ((bf16[8,96,256]{2,1,0:T(8,128)(2,1)}), bf16[8,96,256]{2,1,0:T(8,128)(2,1)S(1)}, u32[]{:S(2)}, u32[]{:S(2)}) async-start(bf16[8,96,256]{2,1,0:T(8,128)(2,1)} %position_conv.1), calls=%async_computation.2 | async-start | bytes 786432 | tf_op jit(solution)/shard_map/all_to_all | solution.py:695
  118.3 14.0 %copy-start.3 = (bf16[768,768]{1,0:T(8,128)(2,1)}, bf16[768,768]{1,0:T(8,128)(2,1)S(1)}, u32[]{:S(2)}) copy-start(bf16[768,768]{1,0:T(8,128)(2,1)S(1)} %slice.265.refs_1_.refs_5_) | copy-start | bytes 3538948
  118.3 28.9 %collective-permute-start.18 = (bf16[768,768]{1,0:T(8,128)(2,1)S(1)}, bf16[768,768]{1,0:T(8,128)(2,1)S(1)}, u32[]{:S(2)}, u32[]{:S(2)}) collective-permute-start(bf16[768,768]{1,0:T(8,128)(2,1)S(1)} %slice.265.refs_1_.refs_5_), channel_id=1, source_target_pairs={{0,2},{1,3},{2,0},{3,1},{4,6},{5,7},{6,4},{7,5},{8,10},{9,11},{10,... | collective-permute-start | bytes 3538952 | tf_op jit(solution)/shard_map/ppermute | solution.py:44
  128.9 21.6 %copy-start.8 = (bf16[8,96,256]{2,1,0:T(8,128)(2,1)}, bf16[8,96,256]{2,1,0:T(8,128)(2,1)S(1)}, u32[]{:S(2)}) copy-start(bf16[8,96,256]{2,1,0:T(8,128)(2,1)S(1)} %all-to-all-done.2) | copy-start | bytes 1179652
  128.9 67.9 %collective-permute-start.21 = (bf16[768,1536]{1,0:T(8,128)(2,1)}, bf16[768,1536]{1,0:T(8,128)(2,1)}, u32[]{:S(2)}, u32[]{:S(2)}) collective-permute-start(bf16[768,1536]{1,0:T(8,128)(2,1)} %slice.263.feed0), channel_id=1, source_target_pairs={{0,2},{1,3},{2,0},{3,1},{4,6},{5,7},{6,4},{7,5},{8,10},{9,11},{10,... | collective-permute-start | bytes 7077896 | tf_op jit(solution)/shard_map/ppermute | solution.py:44
  132.2 18.5 %copy-start.34 = (f32[32,24]{1,0:T(8,128)}, f32[32,24]{1,0:T(8,128)S(1)}, u32[]{:S(2)}) copy-start(f32[32,24]{1,0:T(8,128)S(1)} %get-tuple-element.244) | copy-start | bytes 9220
  132.3 20.4 %collective-permute-start.17 = (bf16[768,768]{1,0:T(8,128)(2,1)S(1)}, bf16[768,768]{1,0:T(8,128)(2,1)}, u32[]{:S(2)}, u32[]{:S(2)}) collective-permute-start(bf16[768,768]{1,0:T(8,128)(2,1)S(1)} %slice.265.refs_1_.refs_5_), channel_id=1, source_target_pairs={{0,1},{1,0},{2,3},{3,2},{4,5},{5,4},{6,7},{7,6},{8,9},{9,8},{10,11... | collective-permute-start | bytes 3538952 | tf_op jit(solution)/shard_map/ppermute | solution.py:44
  147.2 5.5 %collective-permute-start.19 = (bf16[768,768]{1,0:T(8,128)(2,1)S(1)}, bf16[768,768]{1,0:T(8,128)(2,1)}, u32[]{:S(2)}, u32[]{:S(2)}) collective-permute-start(bf16[768,768]{1,0:T(8,128)(2,1)S(1)} %collective-permute-done.18.refs_3_.refs_7_), channel_id=1, source_target_pairs={{0,1},{1,0},{2,3},{3,2},{4,5},{5,4},{6,7},{7,6},{8,9},{9,8},{10,11... | collective-permute-start | bytes 3538952 | tf_op jit(solution)/shard_map/ppermute | solution.py:44
  157.6 48.1 %all-to-all-start.3 = ((bf16[8,576,128]{2,1,0:T(8,128)(2,1)}), bf16[8,576,128]{2,1,0:T(8,128)(2,1)S(1)}, u32[]{:S(2)}, u32[]{:S(2)}) async-start(bf16[8,576,128]{2,1,0:T(8,128)(2,1)} %head_projection.1), calls=%async_computation.3 | async-start | bytes 2359296 | tf_op jit(solution)/shard_map/all_to_all | solution.py:695
  164.0 60.1 %collective-permute-start.20 = (bf16[768,1536]{1,0:T(8,128)(2,1)}, bf16[768,1536]{1,0:T(8,128)(2,1)}, u32[]{:S(2)}, u32[]{:S(2)}) collective-permute-start(bf16[768,1536]{1,0:T(8,128)(2,1)} %slice.263.feed0), channel_id=1, source_target_pairs={{0,1},{1,0},{2,3},{3,2},{4,5},{5,4},{6,7},{7,6},{8,9},{9,8},{10,11... | collective-permute-start | bytes 7077896 | tf_op jit(solution)/shard_map/ppermute | solution.py:44
  196.9 37.0 %collective-permute-start.22 = (bf16[768,1536]{1,0:T(8,128)(2,1)}, bf16[768,1536]{1,0:T(8,128)(2,1)}, u32[]{:S(2)}, u32[]{:S(2)}) collective-permute-start(bf16[768,1536]{1,0:T(8,128)(2,1)} %collective-permute-done.21.feed2), channel_id=1, source_target_pairs={{0,1},{1,0},{2,3},{3,2},{4,5},{5,4},{6,7},{7,6},{8,9},{9,8},{10,11... | collective-permute-start | bytes 7077896 | tf_op jit(solution)/shard_map/ppermute | solution.py:44
  213.3 8.2 %copy-start.37 = (f32[32,24]{1,0:T(8,128)S(1)}, f32[32,24]{1,0:T(8,128)}, u32[]{:S(2)}) copy-start(f32[32,24]{1,0:T(8,128)} %get-tuple-element.243) | copy-start | bytes 9220
  213.3 8.9 %copy-start.36 = (f32[32,24]{1,0:T(8,128)S(1)}, f32[32,24]{1,0:T(8,128)}, u32[]{:S(2)}) copy-start(f32[32,24]{1,0:T(8,128)} %get-tuple-element.242) | copy-start | bytes 9220
  213.3 9.5 %copy-start.12 = (f32[256,768]{0,1:T(8,128)S(1)}, f32[256,768]{0,1:T(8,128)}, u32[]{:S(2)}) copy-start(f32[256,768]{0,1:T(8,128)} %get-tuple-element.180) | copy-start | bytes 2359300
  215.4 18.5 %all-to-all-start.4 = ((bf16[8,192,128]{2,1,0:T(8,128)(2,1)}), bf16[8,192,128]{2,1,0:T(8,128)(2,1)S(1)}, u32[]{:S(2)}, u32[]{:S(2)}) async-start(bf16[8,192,128]{2,1,0:T(8,128)(2,1)} %convert_element_type.252), calls=%async_computation.4 | async-start | bytes 786432 | tf_op jit(solution)/shard_map/all_to_all | solution.py:695
  247.2 15.7 %all-to-all-start.5 = ((bf16[8,192,128]{2,1,0:T(8,128)(2,1)}), bf16[8,192,128]{2,1,0:T(8,128)(2,1)S(1)}, u32[]{:S(2)}, u32[]{:S(2)}) async-start(bf16[8,192,128]{2,1,0:T(8,128)(2,1)} %get-tuple-element.66), calls=%async_computation.5 | async-start | bytes 786432 | tf_op jit(solution)/shard_map/all_to_all | solution.py:695
  281.7 32.5 %all-to-all-start.6 = ((bf16[8,3,192,128]{3,2,1,0:T(8,128)(2,1)}), bf16[8,3,192,128]{3,2,1,0:T(8,128)(2,1)S(1)}, u32[]{:S(2)}, u32[]{:S(2)}) async-start(bf16[8,3,192,128]{3,2,1,0:T(8,128)(2,1)} %copy.229), calls=%async_computation.6 | async-start | bytes 2359296 | tf_op jit(solution)/shard_map/all_to_all | solution.py:695
  285.5 223.5 %reduce-scatter.2.cloned.1.call-start = ((), (), s32[]{:S(2)}) async-start(), calls=%async_computation.14 | async-start | bytes 9732096 | tf_op jit(solution)/shard_map/reduce_scatter | solution.py:843
  316.6 15.3 %collective-permute-start.24 = (bf16[768,768]{0,1:T(8,128)(2,1)}, bf16[768,768]{0,1:T(8,128)(2,1)}, u32[]{:S(2)}, u32[]{:S(2)}) collective-permute-start(bf16[768,768]{0,1:T(8,128)(2,1)} %pad_maximum_fusion.5), channel_id=1, source_target_pairs={{0,1},{1,0},{2,3},{3,2},{4,5},{5,4},{6,7},{7,6},{8,9},{9,8},{10,11... | collective-permute-start | bytes 3538952 | tf_op jit(solution)/shard_map/ppermute | solution.py:44
  318.4 16.2 %collective-permute-start.23 = (bf16[768,768]{0,1:T(8,128)(2,1)}, bf16[768,768]{0,1:T(8,128)(2,1)}, u32[]{:S(2)}, u32[]{:S(2)}) collective-permute-start(bf16[768,768]{0,1:T(8,128)(2,1)} %pad_maximum_fusion.4), channel_id=1, source_target_pairs={{0,1},{1,0},{2,3},{3,2},{4,5},{5,4},{6,7},{7,6},{8,9},{9,8},{10,11... | collective-permute-start | bytes 3538952 | tf_op jit(solution)/shard_map/ppermute | solution.py:44
  327.1 15.8 %all-to-all-start.7 = ((bf16[8,96,256]{2,1,0:T(8,128)(2,1)}), bf16[8,96,256]{2,1,0:T(8,128)(2,1)S(1)}, u32[]{:S(2)}, u32[]{:S(2)}) async-start(bf16[8,96,256]{2,1,0:T(8,128)(2,1)} %bitcast.377), calls=%async_computation.7 | async-start | bytes 786432 | tf_op jit(solution)/shard_map/all_to_all | solution.py:695
  336.2 24.3 %copy-start.15 = (bf16[256,1024]{1,0:T(8,128)(2,1)S(1)}, bf16[256,1024]{1,0:T(8,128)(2,1)}, u32[]{:S(2)}) copy-start(bf16[256,1024]{1,0:T(8,128)(2,1)} %copy-done.14) | copy-start | bytes 1572868
  336.3 24.3 %copy-start.26 = (bf16[256,512]{1,0:T(8,128)(2,1)S(1)}, bf16[256,512]{1,0:T(8,128)(2,1)}, u32[]{:S(2)}) copy-start(bf16[256,512]{1,0:T(8,128)(2,1)} %copy-done.25) | copy-start | bytes 786436
  342.9 33.9 %collective-permute-start.25 = (bf16[768,768]{0,1:T(8,128)(2,1)}, bf16[768,768]{0,1:T(8,128)(2,1)}, u32[]{:S(2)}, u32[]{:S(2)}) collective-permute-start(bf16[768,768]{0,1:T(8,128)(2,1)} %add_convert_fusion.1), channel_id=1, source_target_pairs={{0,2},{1,3},{2,0},{3,1},{4,6},{5,7},{6,4},{7,5},{8,10},{9,11},{10,... | collective-permute-start | bytes 3538952 | tf_op jit(solution)/shard_map/ppermute | solution.py:44
  356.4 26.2 %all-to-all-start.8 = ((bf16[8,96,256]{2,1,0:T(8,128)(2,1)}), bf16[8,96,256]{2,1,0:T(8,128)(2,1)S(1)}, u32[]{:S(2)}, u32[]{:S(2)}) async-start(bf16[8,96,256]{2,1,0:T(8,128)(2,1)} %get-tuple-element.79), calls=%async_computation.8 | async-start | bytes 786432 | tf_op jit(solution)/shard_map/all_to_all | solution.py:695
  391.6 2.2 collective-permute-start.28
  399.7 1.9 collective-permute-start.31
  399.9 31.4 %collective-permute-start.27 = (bf16[8,80,512]{2,1,0:T(8,128)(2,1)S(1)}, bf16[8,80,512]{2,1,0:T(8,128)(2,1)S(1)}, u32[]{:S(2)}, u32[]{:S(2)}) collective-permute-start(bf16[8,80,512]{2,1,0:T(8,128)(2,1)S(1)} %get-tuple-element.196), channel_id=1, source_target_pairs={{0,1},{1,0},{2,3},{3,2},{4,5},{5,4},{6,7},{7,6},{8,9},{9,8},{10,11... | collective-permute-start | bytes 1966088 | tf_op jit(solution)/shard_map/ppermute | solution.py:44
  400.7 30.6 %collective-permute-start.29 = (bf16[8,80,512]{2,1,0:T(8,128)(2,1)S(1)}, bf16[8,80,512]{2,1,0:T(8,128)(2,1)S(1)}, u32[]{:S(2)}, u32[]{:S(2)}) collective-permute-start(bf16[8,80,512]{2,1,0:T(8,128)(2,1)S(1)} %copy-done.27), channel_id=1, source_target_pairs={{0,2},{1,3},{2,0},{3,1},{4,6},{5,7},{6,4},{7,5},{8,10},{9,11},{10,... | collective-permute-start | bytes 1966088 | tf_op jit(solution)/shard_map/ppermute | solution.py:44
  401.6 1.7 collective-permute-start.30
  401.9 28.4 %collective-permute-start.32 = (bf16[1,8,96,192]{3,2,1,0:T(8,128)(2,1)S(1)}, bf16[1,8,96,192]{3,2,1,0:T(8,128)(2,1)S(1)}, u32[]{:S(2)}, u32[]{:S(2)}) collective-permute-start(bf16[1,8,96,192]{3,2,1,0:T(8,128)(2,1)S(1)} %fusion.35), channel_id=1, source_target_pairs={{0,2},{1,3},{2,0},{3,1},{4,6},{5,7},{6,4},{7,5},{8,10},{9,11},{10,... | collective-permute-start | bytes 884744 | tf_op jit(solution)/shard_map/ppermute | solution.py:44
  433.6 15.3 %all-to-all-start.11 = ((bf16[8,96,192]{2,1,0:T(8,128)(2,1)}), bf16[8,96,192]{2,1,0:T(8,128)(2,1)S(1)}, u32[]{:S(2)}, u32[]{:S(2)}) async-start(bf16[8,96,192]{2,1,0:T(8,128)(2,1)} %bitcast.92), calls=%async_computation.11 | async-start | bytes 786432 | tf_op jit(solution)/shard_map/all_to_all | solution.py:695
  481.5 20.4 %all-to-all-start.9 = ((bf16[8,1,80,512]{3,2,1,0:T(8,128)(2,1)}), bf16[8,1,80,512]{3,2,1,0:T(8,128)(2,1)S(1)}, u32[]{:S(2)}, u32[]{:S(2)}) async-start(bf16[8,1,80,512]{3,2,1,0:T(8,128)(2,1)} %bitcast.82), calls=%async_computation.9 | async-start | bytes 1310720 | tf_op jit(solution)/shard_map/all_to_all | solution.py:695
  486.2 5.1 collective-permute-start.26
  502.0 5.2 %collective-permute-start.33 = (f32[24,576]{1,0:T(8,128)S(1)}, f32[24,576]{1,0:T(8,128)S(1)}, u32[]{:S(2)}, u32[]{:S(2)}) collective-permute-start(f32[24,576]{1,0:T(8,128)S(1)} %get-tuple-element.227), channel_id=1, source_target_pairs={{0,1},{1,0},{2,3},{3,2},{4,5},{5,4},{6,7},{7,6},{8,9},{9,8},{10,11... | collective-permute-start | bytes 165896 | tf_op jit(solution)/shard_map/ppermute | solution.py:44
  502.1 5.1 collective-permute-start.34
  502.5 4.9 collective-permute-start.35
  (31 other events, 86.1 us)
Sparse Core Ops, SparseCore 0:
  26.6 80.0 all-gather.1
  292.2 149.9 reduce-scatter.1
where the time goes:
time: 530 us; the launch traced here: 520 us
  waiting for transfers between devices  209 us (39%)
  starting transfers between devices  81.6 us (15%)
  Pallas kernels  79.9 us (15%)
  local copies, waits for them, and re-layouts  58.1 us (11%)
  other arithmetic  38.4 us (7%)
  blocking collectives  32.6 us (6%)
  between operations  15.8 us (3%)
    ppermute x27, waiting for transfers between devices, swapped(): return lax.ppermute(array, 'fsdp', [(i, i ^ k) for i in range(count)])  115 us
    all_to_all x11, waiting for transfers between devices, near_swap(): return lax.all_to_all(blocks, 'seq', 0, 0, axis_index_groups=near)  83.9 us
    all_to_all x11, starting transfers between devices, near_swap(): return lax.all_to_all(blocks, 'seq', 0, 0, axis_index_groups=near)  48.1 us
    all_to_all x1, blocking collectives, near_swap(): return lax.all_to_all(blocks, 'seq', 0, 0, axis_index_groups=near)  32.6 us
    ppermute x27, starting transfers between devices, swapped(): return lax.ppermute(array, 'fsdp', [(i, i ^ k) for i in range(count)])  16.3 us
    pallas_call x1, Pallas kernels, attention_back(): pl.pallas_call(lambda *refs: attention_back_kernel(block, *refs), grid=(h...  15.5 us
    pallas_call x1, Pallas kernels, feed_forward(): pl.pallas_call(feed_kernel, in_specs=[vmem] * 6 + [pl.BlockSpec(memory_sp...  12.6 us
    pallas_call x1, Pallas kernels, position_back(): pl.pallas_call(lambda *refs: position_back_kernel(span, frames, *refs), g...  12.1 us
  transfers between devices with their start and end apart: 49, of which 23 were waited for; matrix products, arithmetic and copies ran while one was open for 17% of the time, Pallas kernels for 10%

commit v1 on v0

--- a/solution.py
+++ b/solution.py
@@ -694,9 +694,11 @@
     def near_swap(blocks):
         return lax.all_to_all(blocks, "seq", 0, 0, axis_index_groups=near)
 
-    def seq_sum(blocks):
+    def seq_blocks(blocks):
         shape = (outer, group, -1, blocks.shape[-1])
-        blocks = near_swap(blocks.reshape(shape).transpose(1, 0, 2, 3))
+        return near_swap(blocks.reshape(shape).transpose(1, 0, 2, 3))
+
+    def seq_total(blocks):
         total = jnp.sum(blocks.astype(F32), axis=0)
         if outer == 1:
             return total[0]
@@ -735,7 +737,12 @@
     front = front_near
     if outer > 1:
         front = lax.all_gather(front, "seq", axis=0, tiled=True, axis_index_groups=far)
-    front = jnp.stack(flip(gather_blocks(front), stream), axis=1)
+    own_rows = position_weight.shape[0]
+    share = D // group
+    taps = near_swap(after(position_weight, front_near).T.reshape(group, share, own_rows))
+    over_x, taps = lax.optimization_barrier((swapped(front, 2), taps))
+    front = [front, swapped(front, 1), over_x, swapped(over_x, 1)]
+    front = jnp.stack(flip(front, stream), axis=1)
     front = front.reshape(devices, -1, C_CNN)
     cut = front_rows[0] + front_rows[1]
     conv_full = front[:, : front_rows[0]].reshape(-1, C_CNN)
@@ -750,10 +757,6 @@
         for i in range(3)
     )
 
-    share = D // group
-    own_rows = position_weight.shape[0]
-    taps = near_swap(after(position_weight, front_near).T.reshape(group, share, own_rows))
-
     out_parts = output_weight.reshape(up_rows, streams, part).transpose(1, 0, 2)
     quarter = jnp.concatenate(
         [parts[:, : 3 * part], out_parts.reshape(-1, part), parts[:, 3 * part :], down_weight],
@@ -795,8 +798,7 @@
 
     window, window_edge = to_groups(projected.astype(BF16).T)
     position = position_conv(window, window_edge, position_full)
-    position, quarter = lax.optimization_barrier((position, quarter))
-    middle = gather_blocks(quarter[:, : 4 * part])
+    middle = gather_blocks(after(quarter[:, : 4 * part], position))
     position = near_swap(position).reshape(D, rows)
     feed, position = lax.optimization_barrier((quarter[:, 4 * part :], position))
     feed = gather_blocks(feed)
@@ -897,7 +899,8 @@
         streams, seqs,
     )
     unfolded_grad = unfolded_grad.reshape(MICROS, frames, 3 * C_CNN)
-    middle_shard = seq_sum(after(middle_sum, front_grads))
+    middle_halves = [seq_blocks(middle_sum[:, : 2 * part])]
+    middle_halves.append(seq_blocks(after(middle_sum[:, 2 * part :], middle_halves[0])))
     following_grad = unfolded_grad[:, :, 2 * C_CNN :] * same_next.astype(F32)
     carried = shifted(following_grad[:, frames - 1 :], "seq", 1)
     even_grad = unfolded_grad[:, :, :C_CNN] + jnp.concatenate(
@@ -907,25 +910,35 @@
     input_grad = input_grad.reshape(MICROS, 1, 2 * frames, C_CNN)
 
     front_pairs = pair_sums([front_grads[k] for k in range(streams)])
+    front_sum = low_sum(front_pairs[0], swapped(front_pairs[1], 2))
     taps_grad = after(taps_grad, front_pairs[1])
-    front_sum = low_sum(front_pairs[0], swapped(front_pairs[1], 2))
-    front_shard = seq_sum(front_sum)
-    front_shard, middle_shard = lax.optimization_barrier((front_shard, middle_shard))
-
     taps_grad = (
         taps_grad.transpose(1, 0, 2)
         .reshape(share, outer, group, streams, own_rows)
         .transpose(3, 1, 2, 0, 4)
     )
     taps_grad = reduce_blocks(flip([taps_grad[j] for j in range(streams)], stream))
-    taps_grad = after(taps_grad, front_sum)
+    front_rows = front_sum.shape[1]
+    front_sum = front_sum.reshape(outer, group, front_rows, C_CNN)
+    half = share // 2
+    taps_rows = jnp.concatenate([taps_grad[:, :, :half], taps_grad[:, :, half:]], axis=3)
+    taps_rows = jnp.pad(taps_rows, ((0, 0),) * 3 + ((0, C_CNN - 2 * own_rows),))
+    last = jnp.concatenate([front_sum, taps_rows], axis=2)
+    last, middle_halves = lax.optimization_barrier((last, middle_halves))
+    last = near_swap(last.transpose(1, 0, 2, 3))
+    front_shard = seq_total(last[:, :, :front_rows])
+    taps_rows = last[:, :, front_rows:]
     if outer > 1:
-        taps_grad = lax.psum_scatter(
-            taps_grad, "seq", scatter_dimension=0, axis_index_groups=far
+        taps_rows = lax.psum_scatter(
+            taps_rows, "seq", scatter_dimension=1, axis_index_groups=far
         )
     else:
-        taps_grad = taps_grad[0]
-    position_shard = near_swap(taps_grad).reshape(D, own_rows).T.astype(F32)
+        taps_rows = taps_rows[:, 0]
+    taps_grad = jnp.concatenate(
+        [taps_rows[:, :, :own_rows], taps_rows[:, :, own_rows : 2 * own_rows]], axis=1
+    )
+    position_shard = taps_grad.reshape(D, own_rows).T.astype(F32)
+    middle_shard = jnp.concatenate([seq_total(half) for half in middle_halves], axis=1)
 
     def unswap(block):
         block = block.reshape(streams, up_rows, -1)

time: 530 us -> 506 us (0.955)
  the two profiles are of different devices: /device:TPU:0 before, /device:TPU:16 now
where the time goes in v1:
time: 506 us; the launch traced here: 498 us
  waiting for transfers between devices  181 us (36%)
  starting transfers between devices  115 us (23%)
  Pallas kernels  79.8 us (16%)
  local copies, waits for them, and re-layouts  57.7 us (11%)
  other arithmetic  42.4 us (8%)
  between operations  15.8 us (3%)
  matrix products  6.05 us (1%)
    all_to_all x12, starting transfers between devices, near_swap(): return lax.all_to_all(blocks, 'seq', 0, 0, axis_index_groups=near)  82.4 us
    ppermute x27, waiting for transfers between devices, swapped(): return lax.ppermute(array, 'fsdp', [(i, i ^ k) for i in range(count)])  76.5 us
    all_to_all x12, waiting for transfers between devices, near_swap(): return lax.all_to_all(blocks, 'seq', 0, 0, axis_index_groups=near)  75.6 us
    ppermute x2, waiting for transfers between devices, shifted(): return lax.ppermute(array, axis, pairs)  20 us
    ppermute x27, starting transfers between devices, swapped(): return lax.ppermute(array, 'fsdp', [(i, i ^ k) for i in range(count)])  15.7 us
    pallas_call x1, Pallas kernels, attention_back(): pl.pallas_call(lambda *refs: attention_back_kernel(block, *refs), grid=(h...  15.5 us
    pallas_call x1, Pallas kernels, feed_forward(): pl.pallas_call(feed_kernel, in_specs=[vmem] * 6 + [pl.BlockSpec(memory_sp...  12.6 us
    pallas_call x1, Pallas kernels, position_back(): pl.pallas_call(lambda *refs: position_back_kernel(span, frames, *refs), g...  12.2 us
  transfers between devices with their start and end apart: 50, of which 21 were waited for; matrix products, arithmetic and copies ran while one was open for 18% of the time, Pallas kernels for 10%

profile of v1, /device:TPU:16, one launch (start us, length us, event | category | flops | bytes accessed | tf_op | source)
XLA Modules:
  0.0 497.9 jit_solution(2441230174090456664)
XLA Ops:
  10.2 1.6 collective-permute-start.7
  12.5 1.6 collective-permute-start.1
  14.1 1.6 collective-permute-start.2
  16.3 4.0 collective-permute-start.10
  21.5 1.6 collective-permute-start.9
  24.2 6.7 %collective-permute-done.10 = bf16[80,512]{1,0:T(8,128)(2,1)S(1)} collective-permute-done((bf16[80,512]{1,0:T(8,128)(2,1)S(1)}, bf16[80,512]{1,0:T(8,128)(2,1)S(1)}, u32[]{:S(2)}, u32[]{:S(2)}) %collective-permute-start.10) | collective-permute-done | bytes 81952 | tf_op jit(solution)/shard_map/ppermute | solution.py:711
  30.9 1.7 collective-permute-done.9
  33.5 1.6 collective-permute-start.12
  36.0 5.2 %all-to-all-start = ((bf16[8,96,192]{2,1,0:T(8,128)(2,1)}), bf16[8,96,192]{2,1,0:T(8,128)(2,1)S(1)}, u32[]{:S(2)}, u32[]{:S(2)}) async-start(bf16[8,96,192]{2,1,0:T(8,128)(2,1)} %bitcast.19), calls=%async_computation | async-start | bytes 786432 | tf_op jit(solution)/shard_map/all_to_all | solution.py:695
  41.4 3.4 collective-permute-start
  45.7 11.7 %all-to-all-done = bf16[8,96,192]{2,1,0:T(8,128)(2,1)S(1)} async-done(((bf16[8,96,192]{2,1,0:T(8,128)(2,1)}), bf16[8,96,192]{2,1,0:T(8,128)(2,1)S(1)}, u32[]{:S(2)}, u32[]{:S(2)}) %all-to-all-start) | async-done | bytes 294944 | tf_op jit(solution)/shard_map/all_to_all | solution.py:695
  59.7 1.6 select_bitcast_fusion.3
  63.1 3.5 fusion.75
  70.3 6.9 %all-to-all-start.1 = ((bf16[8,96,256]{2,1,0:T(8,128)(2,1)}), bf16[8,96,256]{2,1,0:T(8,128)(2,1)S(1)}, u32[]{:S(2)}, u32[]{:S(2)}) async-start(bf16[8,96,256]{2,1,0:T(8,128)(2,1)} %bitcast.32), calls=%async_computation.1 | async-start | bytes 786432 | tf_op jit(solution)/shard_map/all_to_all | solution.py:695
  77.2 2.4 collective-permute-done.15
  80.4 6.5 %collective-permute-done.16 = bf16[1,8,96,192]{3,2,1,0:T(8,128)(2,1)} collective-permute-done((bf16[1,8,96,192]{3,2,1,0:T(8,128)(2,1)S(1)}, bf16[1,8,96,192]{3,2,1,0:T(8,128)(2,1)}, u32[]{:S(2)}, u32[]{:S(2)}) %collective-permute-start.16) | collective-permute-done | bytes 294944 | tf_op jit(solution)/shard_map/ppermute | solution.py:44
  89.8 2.3 reshape.607
  92.1 4.0 all-to-all-done.1.refs_0_
  96.9 6.2 %position_conv.1 = bf16[8,96,256]{2,1,0:T(8,128)(2,1)} custom-call(bf16[8,96,256]{2,1,0:T(8,128)(2,1)} %copy-done.11, bf16[96,256]{1,0:T(8,128)(2,1)} %broadcast_7_refs_1__refs_3_.2.refs_1_.refs_3_, bf16[8,96,768]{2,1,0:T(8,128)(2,1)} %bitcast.348), custom_call_target="tpu_custom_call" | custom-call | tf_op jit(solution)/shard_map/position_conv/pallas_call | solution.py:189
  103.1 7.6 %all-to-all-start.2 = ((bf16[8,96,256]{2,1,0:T(8,128)(2,1)}), bf16[8,96,256]{2,1,0:T(8,128)(2,1)S(1)}, u32[]{:S(2)}, u32[]{:S(2)}) async-start(bf16[8,96,256]{2,1,0:T(8,128)(2,1)} %position_conv.1), calls=%async_computation.2 | async-start | bytes 786432 | tf_op jit(solution)/shard_map/all_to_all | solution.py:695
  112.1 1.5 collective-permute-start.18
  113.6 3.3 slice.379.feed0
  116.8 3.8 all-to-all-done.2
  120.6 1.5 collective-permute-start.21
  124.0 17.0 %collective-permute-done.18.refs_3_.refs_7_ = bf16[768,768]{1,0:T(8,128)(2,1)S(1)} collective-permute-done((bf16[768,768]{1,0:T(8,128)(2,1)S(1)}, bf16[768,768]{1,0:T(8,128)(2,1)S(1)}, u32[]{:S(2)}, u32[]{:S(2)}) %collective-permute-start.18) | collective-permute-done | bytes 1179680 | tf_op jit(solution)/shard_map/ppermute | solution.py:44
  141.0 3.3 fusion.73
  146.5 5.0 %head_projection.1 = bf16[8,576,128]{2,1,0:T(8,128)(2,1)} custom-call(bf16[256,768]{1,0:T(8,128)(2,1)} %copy.220.refs_0_, bf16[768,768]{1,0:T(8,128)(2,1)} %copy-done.1, bf16[768,768]{1,0:T(8,128)(2,1)} %collective-permute-done.17.refs_2_.refs_6_, bf16[768,768]{1,0:T(8,128)(2,1)} %copy-done.5, bf16[768,768]{1,0:T(8,128)(2,1)} %collective-permute-done.19.refs_4_.refs_8_), custom_call_target="tpu_custom_call" | custom-call | tf_op jit(solution)/shard_map/head_projection/pallas_call | solution.py:545
  151.5 6.4 %all-to-all-start.3 = ((bf16[8,576,128]{2,1,0:T(8,128)(2,1)}), bf16[8,576,128]{2,1,0:T(8,128)(2,1)S(1)}, u32[]{:S(2)}, u32[]{:S(2)}) async-start(bf16[8,576,128]{2,1,0:T(8,128)(2,1)} %head_projection.1), calls=%async_computation.3 | async-start | bytes 2359296 | tf_op jit(solution)/shard_map/all_to_all | solution.py:695
  158.0 32.1 %collective-permute-done.21.feed2 = bf16[768,1536]{1,0:T(8,128)(2,1)} collective-permute-done((bf16[768,1536]{1,0:T(8,128)(2,1)}, bf16[768,1536]{1,0:T(8,128)(2,1)}, u32[]{:S(2)}, u32[]{:S(2)}) %collective-permute-start.21) | collective-permute-done | bytes 2359328 | tf_op jit(solution)/shard_map/ppermute | solution.py:44
  191.3 2.0 select_select_fusion.11
  199.9 6.5 %attention.1.refs_4_ = f32[8,192,128]{2,1,0:T(8,128)} custom-call(bf16[8,3,192,128]{3,2,1,0:T(8,128)(2,1)} %bitcast.336, bf16[8,3,192,128]{3,2,1,0:T(8,128)(2,1)} %bitcast.337, bf16[8,3,192,128]{3,2,1,0:T(8,128)(2,1)} %bitcast.338, s32[1024,1]{1,0:T(8,128)} %copy.225.refs_3_.refs_6_, s32[1,1024]{1,0:T(1,128)} %bitcast.401), custom_call_target="tpu_custom_call" | custom-call | tf_op jit(solution)/shard_map/attention/pallas_call | solution.py:320
  206.4 2.1 convert_element_type.257
  208.5 6.5 %all-to-all-start.4 = ((bf16[8,192,128]{2,1,0:T(8,128)(2,1)}), bf16[8,192,128]{2,1,0:T(8,128)(2,1)S(1)}, u32[]{:S(2)}, u32[]{:S(2)}) async-start(bf16[8,192,128]{2,1,0:T(8,128)(2,1)} %convert_element_type.257), calls=%async_computation.4 | async-start | bytes 786432 | tf_op jit(solution)/shard_map/all_to_all | solution.py:695
  217.5 7.3 %all-to-all-done.4.ctx_ref = bf16[8,192,128]{2,1,0:T(8,128)(2,1)S(1)} async-done(((bf16[8,192,128]{2,1,0:T(8,128)(2,1)}), bf16[8,192,128]{2,1,0:T(8,128)(2,1)S(1)}, u32[]{:S(2)}, u32[]{:S(2)}) %all-to-all-start.4) | async-done | bytes 393248 | tf_op jit(solution)/shard_map/all_to_all | solution.py:695
  225.6 12.6 %feed_forward.1 = (f32[256,768]{1,0:T(8,128)}, f32[256,768]{1,0:T(8,128)}, bf16[8,192,128]{2,1,0:T(8,128)(2,1)}, f32[1,768]{1,0:T(1,128)}, f32[1,768]{1,0:T(1,12...) custom-call(bf16[8,192,128]{2,1,0:T(8,128)(2,1)} %copy-done.9, ...), custom_call_target="tpu_custom_call" | custom-call | tf_op jit(solution)/shard_map/feed_forward/pallas_call | solution.py:469
  238.2 6.3 %all-to-all-start.5 = ((bf16[8,192,128]{2,1,0:T(8,128)(2,1)}), bf16[8,192,128]{2,1,0:T(8,128)(2,1)S(1)}, u32[]{:S(2)}, u32[]{:S(2)}) async-start(bf16[8,192,128]{2,1,0:T(8,128)(2,1)} %get-tuple-element.68), calls=%async_computation.5 | async-start | bytes 786432 | tf_op jit(solution)/shard_map/all_to_all | solution.py:695
  244.6 8.5 %feed_grad.1 = bf16[8,4,2,4,24,768]{5,4,3,2,1,0:T(8,128)(2,1)} custom-call(s32[1]{0:T(128)} %bitcast.55.stream_ref, bf16[256,768]{1,0:T(8,128)(2,1)} %get-tuple-element.69.settled_ref, bf16[256,3072]{1,0:T(8,128)(2,1)} %get-tuple-element.70.up_ref, bf16[256,3072]{1,0:T(8,128)(2,1)} %get-tuple-element.71.hidden_ref, bf16[256,768]{1,0:T(8,128)(2,1)} %get-tuple-element.72.fed_ref), custom_call_target="tpu_custom_call" | custom-call | tf_op jit(solution)/shard_map/feed_grad/pallas_call | solution.py:520
  254.8 15.5 %attention_back.1 = (bf16[8,192,128]{2,1,0:T(8,128)(2,1)}, bf16[8,192,128]{2,1,0:T(8,128)(2,1)}, bf16[8,192,128]{2,1,0:T(8,128)(2,1)}) custom-call(bf16[8,3,192,128]{3,2,1,0:T(8,128)(2,1)} %bitcast.339, bf16[8,3,192,128]{3,2,1,0:T(8,128)(2,1)} %bitcast.340, bf16[8,3,192,128]{3,2,1,0:T(8,128)(2,1)} %bitcast.341, bf16[8,192,128]{2,1,0:T(8,128)(2,1)} %copy-done.18, ...), custom_call_target="tpu_custom_call" | custom-call | tf_op jit(solution)/shard_map/attention_back/pallas_call | solution.py:344
  272.7 6.1 %all-to-all-start.6 = ((bf16[8,3,192,128]{3,2,1,0:T(8,128)(2,1)}), bf16[8,3,192,128]{3,2,1,0:T(8,128)(2,1)S(1)}, u32[]{:S(2)}, u32[]{:S(2)}) async-start(bf16[8,3,192,128]{3,2,1,0:T(8,128)(2,1)} %copy.228), calls=%async_computation.6 | async-start | bytes 2359296 | tf_op jit(solution)/shard_map/all_to_all | solution.py:695
  282.3 3.5 reshape.615
  286.6 17.7 %all-to-all-done.6 = bf16[8,3,192,128]{3,2,1,0:T(8,128)(2,1)S(1)} async-done(((bf16[8,3,192,128]{3,2,1,0:T(8,128)(2,1)}), bf16[8,3,192,128]{3,2,1,0:T(8,128)(2,1)S(1)}, u32[]{:S(2)}, u32[]{:S(2)}) %all-to-all-start.6) | async-done | bytes 1179680 | tf_op jit(solution)/shard_map/all_to_all | solution.py:695
  310.5 6.6 %head_back.1 = (f32[256,768]{1,0:T(8,128)}, bf16[768,256]{1,0:T(8,128)(2,1)}, f32[1,768]{1,0:T(1,128)}) custom-call(bf16[8,576,128]{2,1,0:T(8,128)(2,1)} %bitcast.347, f32[256,768]{1,0:T(8,128)} %get-tuple-element.77.refs_1_, bf16[768,256]{1,0:T(8,128)(2,1)} %bitcast.357, f32[256,768]{1,0:T(8,128)} %copy-done.2, f32[1,768]{1,0:T(1,128)} %reshape.631.refs_4_, ...), custom_call_target="tpu_custom_call" | custom-call | tf_op jit(solution)/shard_map/head_back/pallas_call | solution.py:575
  317.0 7.2 %all-to-all-start.7 = ((bf16[8,96,256]{2,1,0:T(8,128)(2,1)}), bf16[8,96,256]{2,1,0:T(8,128)(2,1)S(1)}, u32[]{:S(2)}, u32[]{:S(2)}) async-start(bf16[8,96,256]{2,1,0:T(8,128)(2,1)} %bitcast.394), calls=%async_computation.7 | async-start | bytes 786432 | tf_op jit(solution)/shard_map/all_to_all | solution.py:695
  325.1 2.6 add_convert_fusion.1
  327.7 1.7 add_convert_fusion.2
  329.4 4.3 all-to-all-done.7.refs_2_
  333.7 1.5 collective-permute-start.25
  335.2 12.2 %position_back.1 = (bf16[8,96,256]{2,1,0:T(8,128)(2,1)}, bf16[8,96,768]{2,1,0:T(8,128)(2,1)}) custom-call(bf16[8,96,256]{2,1,0:T(8,128)(2,1)} %copy-done.11, bf16[96,256]{1,0:T(8,128)(2,1)} %broadcast_7_refs_1__refs_3_.2.refs_1_.refs_3_, bf16[8,96,256]{2,1,0:T(8,128)(2,1)} %copy-done.19, bf16[96,256]{1,0:T(8,128)(2,1)} %broadcast_7_refs_1__refs_3_.2.refs_1_.refs_3_, ...), custom_call_target="tpu_custom_call" | custom-call | tf_op jit(solution)/shard_map/position_back/pallas_call | solution.py:208
  347.4 6.1 %all-to-all-start.8 = ((bf16[8,96,256]{2,1,0:T(8,128)(2,1)}), bf16[8,96,256]{2,1,0:T(8,128)(2,1)S(1)}, u32[]{:S(2)}, u32[]{:S(2)}) async-start(bf16[8,96,256]{2,1,0:T(8,128)(2,1)} %get-tuple-element.81), calls=%async_computation.8 | async-start | bytes 786432 | tf_op jit(solution)/shard_map/all_to_all | solution.py:695
  355.1 15.0 %collective-permute-done.25 = bf16[768,768]{0,1:T(8,128)(2,1)} collective-permute-done((bf16[768,768]{0,1:T(8,128)(2,1)}, bf16[768,768]{0,1:T(8,128)(2,1)}, u32[]{:S(2)}, u32[]{:S(2)}) %collective-permute-start.25) | collective-permute-done | bytes 1179680 | tf_op jit(solution)/shard_map/ppermute | solution.py:44
  370.1 1.6 add_convert_fusion
  372.5 6.7 %front_back.1 = (bf16[4,8,80,512]{3,2,1,0:T(8,128)(2,1)}, f32[256,1536]{1,0:T(8,128)}) custom-call(s32[1]{0:T(128)} %bitcast.55.stream_ref, bf16[768,256]{1,0:T(8,128)(2,1)} %bitcast.372, f32[256,768]{1,0:T(8,128)} %get-tuple-element.85.joined_ref, bf16[256,512]{1,0:T(8,128)(2,1)} %copy-done.13, bf16[512,768]{1,0:T(8,128)(2,1)} %copy-done.4, ...), custom_call_target="tpu_custom_call" | custom-call | tf_op jit(solution)/shard_map/front_back/pallas_call | solution.py:648
  379.1 2.2 slice_bitcast_fusion.1
  383.3 7.7 %all-to-all-start.9 = ((bf16[8,1,96,384]{3,2,1,0:T(8,128)(2,1)}), bf16[8,1,96,384]{3,2,1,0:T(8,128)(2,1)}, u32[]{:S(2)}, u32[]{:S(2)}) async-start(bf16[8,1,96,384]{3,2,1,0:T(8,128)(2,1)} %bitcast.89), calls=%async_computation.9 | async-start | bytes 1179648 | tf_op jit(solution)/shard_map/all_to_all | solution.py:695
  391.0 2.1 fusion
  396.2 1.7 collective-permute-done.31
  401.0 11.2 %all-to-all-done.9 = bf16[8,1,96,384]{3,2,1,0:T(8,128)(2,1)} async-done(((bf16[8,1,96,384]{3,2,1,0:T(8,128)(2,1)}), bf16[8,1,96,384]{3,2,1,0:T(8,128)(2,1)}, u32[]{:S(2)}, u32[]{:S(2)}) %all-to-all-start.9) | async-done | bytes 589856 | tf_op jit(solution)/shard_map/all_to_all | solution.py:695
  413.2 9.6 %all-to-all-start.10 = ((bf16[8,1,96,384]{3,2,1,0:T(8,128)(2,1)}), bf16[8,1,96,384]{3,2,1,0:T(8,128)(2,1)S(1)}, u32[]{:S(2)}, u32[]{:S(2)}) async-start(bf16[8,1,96,384]{3,2,1,0:T(8,128)(2,1)} %bitcast.91), calls=%async_computation.10 | async-start | bytes 1179648 | tf_op jit(solution)/shard_map/all_to_all | solution.py:695
  424.5 1.6 fusion.39
  427.1 14.8 %all-to-all-done.10 = bf16[8,1,96,384]{3,2,1,0:T(8,128)(2,1)S(1)} async-done(((bf16[8,1,96,384]{3,2,1,0:T(8,128)(2,1)}), bf16[8,1,96,384]{3,2,1,0:T(8,128)(2,1)S(1)}, u32[]{:S(2)}, u32[]{:S(2)}) %all-to-all-start.10) | async-done | bytes 589856 | tf_op jit(solution)/shard_map/all_to_all | solution.py:695
  442.0 6.7 %all-to-all-start.11 = ((bf16[8,1,128,512]{3,2,1,0:T(8,128)(2,1)}), bf16[8,1,128,512]{3,2,1,0:T(8,128)(2,1)S(1)}, u32[]{:S(2)}, u32[]{:S(2)}) async-start(bf16[8,1,128,512]{3,2,1,0:T(8,128)(2,1)} %bitcast.93), calls=%async_computation.11 | async-start | bytes 2097152 | tf_op jit(solution)/shard_map/all_to_all | solution.py:695
  449.8 3.4 collective-permute-start.26
  453.2 20.0 %collective-permute-done.26 = f32[2,1,512]{2,1,0:T(1,128)S(1)} collective-permute-done((f32[2,1,512]{2,1,0:T(1,128)S(1)}, f32[2,1,512]{2,1,0:T(1,128)S(1)}, u32[]{:S(2)}, u32[]{:S(2)}) %collective-permute-start.26) | collective-permute-done | bytes 4128 | tf_op jit(solution)/shard_map/ppermute | solution.py:34
  476.1 2.1 collective-permute-start.34
  (314 shorter events, 83.6 us)
Async XLA Ops:
  7.2 103.5 %all-gather.2.cloned.1.call-start = ((), (), s32[]{:S(2)}) async-start(), calls=%async_computation.13 | async-start | bytes 3981312 | tf_op jit(solution)/shard_map/all_gather | solution.py:765
  9.8 13.2 %copy-start.37 = (bf16[24,768]{1,0:T(8,128)(2,1)S(1)}, bf16[24,768]{1,0:T(8,128)(2,1)}, u32[]{:S(2)}) copy-start(bf16[24,768]{1,0:T(8,128)(2,1)} %param.28) | copy-start | bytes 110596
  10.1 13.2 %copy-start.29 = (bf16[96,768]{1,0:T(8,128)(2,1)S(1)}, bf16[96,768]{1,0:T(8,128)(2,1)}, u32[]{:S(2)}) copy-start(bf16[96,768]{1,0:T(8,128)(2,1)} %param.31) | copy-start | bytes 442372
  10.1 5.6 %collective-permute-start.5 = (bf16[24,1344]{1,0:T(8,128)(2,1)S(1)}, bf16[24,1344]{1,0:T(8,128)(2,1)S(1)}, u32[]{:S(2)}, u32[]{:S(2)}) collective-permute-start(bf16[24,1344]{1,0:T(8,128)(2,1)S(1)} %get-tuple-element.243), channel_id=1, source_target_pairs={{0,1},{1,0},{2,3},{3,2},{4,5},{5,4},{6,7},{7,6},{8,9},{9,8},{10,11... | collective-permute-start | bytes 193544 | tf_op jit(solution)/shard_map/ppermute | solution.py:44
  10.2 5.9 %collective-permute-start.7 = (bf16[24,1344]{1,0:T(8,128)(2,1)S(1)}, bf16[24,1344]{1,0:T(8,128)(2,1)S(1)}, u32[]{:S(2)}, u32[]{:S(2)}) collective-permute-start(bf16[24,1344]{1,0:T(8,128)(2,1)S(1)} %get-tuple-element.242), channel_id=1, source_target_pairs={{0,3},{1,2},{2,1},{3,0},{4,7},{5,6},{6,5},{7,4},{8,11},{9,10},{10,... | collective-permute-start | bytes 193544 | tf_op jit(solution)/shard_map/ppermute | solution.py:44
  11.8 4.3 collective-permute-start.6
  12.5 7.7 %collective-permute-start.1 = (bf16[80,512]{1,0:T(8,128)(2,1)S(1)}, bf16[80,512]{1,0:T(8,128)(2,1)S(1)}, u32[]{:S(2)}, u32[]{:S(2)}) collective-permute-start(bf16[80,512]{1,0:T(8,128)(2,1)S(1)} %fusion.61), channel_id=1, source_target_pairs={{0,4},{4,0},{8,12},{12,8},{16,20},{20,16},{24,28},{28,24},{1,5},{5... | collective-permute-start | bytes 245768 | tf_op jit(solution)/shard_map/ppermute | solution.py:711
  14.1 7.3 %collective-permute-start.2 = (bf16[80,512]{1,0:T(8,128)(2,1)S(1)}, bf16[80,512]{1,0:T(8,128)(2,1)S(1)}, u32[]{:S(2)}, u32[]{:S(2)}) collective-permute-start(bf16[80,512]{1,0:T(8,128)(2,1)S(1)} %fusion.61), channel_id=1, source_target_pairs={{0,8},{4,12},{8,0},{12,4},{16,24},{20,28},{24,16},{28,20},{1,9},{5... | collective-permute-start | bytes 245768 | tf_op jit(solution)/shard_map/ppermute | solution.py:711
  15.7 8.5 %collective-permute-start.3 = (bf16[80,512]{1,0:T(8,128)(2,1)S(1)}, bf16[80,512]{1,0:T(8,128)(2,1)S(1)}, u32[]{:S(2)}, u32[]{:S(2)}) collective-permute-start(bf16[80,512]{1,0:T(8,128)(2,1)S(1)} %fusion.61), channel_id=1, source_target_pairs={{0,12},{4,8},{8,4},{12,0},{16,28},{20,24},{24,20},{28,16},{1,13},{... | collective-permute-start | bytes 245768 | tf_op jit(solution)/shard_map/ppermute | solution.py:711
  16.1 8.1 %collective-permute-start.4 = (bf16[80,512]{1,0:T(8,128)(2,1)S(1)}, bf16[80,512]{1,0:T(8,128)(2,1)S(1)}, u32[]{:S(2)}, u32[]{:S(2)}) collective-permute-start(bf16[80,512]{1,0:T(8,128)(2,1)S(1)} %fusion.61), channel_id=1, source_target_pairs={{0,16},{4,20},{8,24},{12,28},{16,0},{20,4},{24,8},{28,12},{1,17},{... | collective-permute-start | bytes 245768 | tf_op jit(solution)/shard_map/ppermute | solution.py:711
  16.3 14.7 %collective-permute-start.10 = (bf16[80,512]{1,0:T(8,128)(2,1)S(1)}, bf16[80,512]{1,0:T(8,128)(2,1)S(1)}, u32[]{:S(2)}, u32[]{:S(2)}) collective-permute-start(bf16[80,512]{1,0:T(8,128)(2,1)S(1)} %fusion.61), channel_id=1, source_target_pairs={{0,28},{4,24},{8,20},{12,16},{16,12},{20,8},{24,4},{28,0},{1,29},{... | collective-permute-start | bytes 245768 | tf_op jit(solution)/shard_map/ppermute | solution.py:711
  20.3 10.7 %collective-permute-start.8 = (bf16[80,512]{1,0:T(8,128)(2,1)S(1)}, bf16[80,512]{1,0:T(8,128)(2,1)S(1)}, u32[]{:S(2)}, u32[]{:S(2)}) collective-permute-start(bf16[80,512]{1,0:T(8,128)(2,1)S(1)} %fusion.61), channel_id=1, source_target_pairs={{0,20},{4,16},{8,28},{12,24},{16,4},{20,0},{24,12},{28,8},{1,21},{... | collective-permute-start | bytes 245768 | tf_op jit(solution)/shard_map/ppermute | solution.py:711
  21.5 11.2 %collective-permute-start.9 = (bf16[80,512]{1,0:T(8,128)(2,1)S(1)}, bf16[80,512]{1,0:T(8,128)(2,1)S(1)}, u32[]{:S(2)}, u32[]{:S(2)}) collective-permute-start(bf16[80,512]{1,0:T(8,128)(2,1)S(1)} %fusion.61), channel_id=1, source_target_pairs={{0,24},{4,28},{8,16},{12,20},{16,8},{20,12},{24,0},{28,4},{1,25},{... | collective-permute-start | bytes 245768 | tf_op jit(solution)/shard_map/ppermute | solution.py:711
  33.4 11.5 %copy-start.41 = (s32[2,1,12]{2,1,0:T(1,128)S(1)}, s32[2,1,12]{2,1,0:T(1,128)}, u32[]{:S(2)}) copy-start(s32[2,1,12]{2,1,0:T(1,128)} %param.21) | copy-start | bytes 292
  33.5 24.0 %collective-permute-start.12 = (bf16[8,80,512]{2,1,0:T(8,128)(2,1)S(1)}, bf16[8,80,512]{2,1,0:T(8,128)(2,1)S(1)}, u32[]{:S(2)}, u32[]{:S(2)}) collective-permute-start(bf16[8,80,512]{2,1,0:T(8,128)(2,1)S(1)} %bitcast_dynamic-update-slice_fusion), channel_id=1, source_target_pairs={{0,2},{1,3},{2,0},{3,1},{4,6},{5,7},{6,4},{7,5},{8,10},{9,11},{10,... | collective-permute-start | bytes 1966088 | tf_op jit(solution)/shard_map/ppermute | solution.py:44
  36.0 21.4 %all-to-all-start = ((bf16[8,96,192]{2,1,0:T(8,128)(2,1)}), bf16[8,96,192]{2,1,0:T(8,128)(2,1)S(1)}, u32[]{:S(2)}, u32[]{:S(2)}) async-start(bf16[8,96,192]{2,1,0:T(8,128)(2,1)} %bitcast.19), calls=%async_computation | async-start | bytes 786432 | tf_op jit(solution)/shard_map/all_to_all | solution.py:695
  41.4 17.1 %collective-permute-start = (bf16[2,1,512]{2,1,0:T(2,128)(2,1)S(1)}, bf16[2,1,512]{2,1,0:T(2,128)(2,1)S(1)}, u32[]{:S(2)}, u32[]{:S(2)}) collective-permute-start(bf16[2,1,512]{2,1,0:T(2,128)(2,1)S(1)} %slice.366), channel_id=1, source_target_pairs={{4,0},{8,4},{12,8},{16,12},{20,16},{24,20},{28,24},{5,1},{9,5},{13... | collective-permute-start | bytes 6152 | tf_op jit(solution)/shard_map/ppermute | solution.py:34
  45.7 13.7 %collective-permute-start.11 = (bf16[8,80,512]{2,1,0:T(8,128)(2,1)S(1)}, bf16[8,80,512]{2,1,0:T(8,128)(2,1)}, u32[]{:S(2)}, u32[]{:S(2)}) collective-permute-start(bf16[8,80,512]{2,1,0:T(8,128)(2,1)S(1)} %bitcast_dynamic-update-slice_fusion), channel_id=1, source_target_pairs={{0,1},{1,0},{2,3},{3,2},{4,5},{5,4},{6,7},{7,6},{8,9},{9,8},{10,11... | collective-permute-start | bytes 1966088 | tf_op jit(solution)/shard_map/ppermute | solution.py:44
  57.4 2.2 collective-permute-start.13
  67.4 54.6 %copy-start.2 = (f32[256,768]{1,0:T(8,128)}, f32[256,768]{1,0:T(8,128)S(1)}, u32[]{:S(2)}) copy-start(f32[256,768]{1,0:T(8,128)S(1)} %fusion.85.refs_3_) | copy-start | bytes 2359300
  67.4 9.8 %collective-permute-start.14 = (bf16[1,8,96,192]{3,2,1,0:T(8,128)(2,1)S(1)}, bf16[1,8,96,192]{3,2,1,0:T(8,128)(2,1)S(1)}, u32[]{:S(2)}, u32[]{:S(2)}) collective-permute-start(bf16[1,8,96,192]{3,2,1,0:T(8,128)(2,1)S(1)} %bitcast.366), channel_id=1, source_target_pairs={{0,1},{1,0},{2,3},{3,2},{4,5},{5,4},{6,7},{7,6},{8,9},{9,8},{10,11... | collective-permute-start | bytes 884744 | tf_op jit(solution)/shard_map/ppermute | solution.py:44
  67.7 11.9 %collective-permute-start.15 = (bf16[1,8,96,192]{3,2,1,0:T(8,128)(2,1)S(1)}, bf16[1,8,96,192]{3,2,1,0:T(8,128)(2,1)S(1)}, u32[]{:S(2)}, u32[]{:S(2)}) collective-permute-start(bf16[1,8,96,192]{3,2,1,0:T(8,128)(2,1)S(1)} %bitcast.367), channel_id=1, source_target_pairs={{0,2},{1,3},{2,0},{3,1},{4,6},{5,7},{6,4},{7,5},{8,10},{9,11},{10,... | collective-permute-start | bytes 884744 | tf_op jit(solution)/shard_map/ppermute | solution.py:44
  69.1 17.7 %collective-permute-start.16 = (bf16[1,8,96,192]{3,2,1,0:T(8,128)(2,1)S(1)}, bf16[1,8,96,192]{3,2,1,0:T(8,128)(2,1)}, u32[]{:S(2)}, u32[]{:S(2)}) collective-permute-start(bf16[1,8,96,192]{3,2,1,0:T(8,128)(2,1)S(1)} %bitcast.368), channel_id=1, source_target_pairs={{0,3},{1,2},{2,1},{3,0},{4,7},{5,6},{6,5},{7,4},{8,11},{9,10},{10,... | collective-permute-start | bytes 884744 | tf_op jit(solution)/shard_map/ppermute | solution.py:44
  70.3 25.8 %all-to-all-start.1 = ((bf16[8,96,256]{2,1,0:T(8,128)(2,1)}), bf16[8,96,256]{2,1,0:T(8,128)(2,1)S(1)}, u32[]{:S(2)}, u32[]{:S(2)}) async-start(bf16[8,96,256]{2,1,0:T(8,128)(2,1)} %bitcast.32), calls=%async_computation.1 | async-start | bytes 786432 | tf_op jit(solution)/shard_map/all_to_all | solution.py:695
  103.1 17.5 %all-to-all-start.2 = ((bf16[8,96,256]{2,1,0:T(8,128)(2,1)}), bf16[8,96,256]{2,1,0:T(8,128)(2,1)S(1)}, u32[]{:S(2)}, u32[]{:S(2)}) async-start(bf16[8,96,256]{2,1,0:T(8,128)(2,1)} %position_conv.1), calls=%async_computation.2 | async-start | bytes 786432 | tf_op jit(solution)/shard_map/all_to_all | solution.py:695
  112.0 11.9 %copy-start.1 = (bf16[768,768]{1,0:T(8,128)(2,1)}, bf16[768,768]{1,0:T(8,128)(2,1)S(1)}, u32[]{:S(2)}) copy-start(bf16[768,768]{1,0:T(8,128)(2,1)S(1)} %slice.381.refs_1_.refs_5_) | copy-start | bytes 3538948
  112.1 29.0 %collective-permute-start.18 = (bf16[768,768]{1,0:T(8,128)(2,1)S(1)}, bf16[768,768]{1,0:T(8,128)(2,1)S(1)}, u32[]{:S(2)}, u32[]{:S(2)}) collective-permute-start(bf16[768,768]{1,0:T(8,128)(2,1)S(1)} %slice.381.refs_1_.refs_5_), channel_id=1, source_target_pairs={{0,2},{1,3},{2,0},{3,1},{4,6},{5,7},{6,4},{7,5},{8,10},{9,11},{10,... | collective-permute-start | bytes 3538952 | tf_op jit(solution)/shard_map/ppermute | solution.py:44
  120.6 23.8 %copy-start.8 = (bf16[8,96,256]{2,1,0:T(8,128)(2,1)}, bf16[8,96,256]{2,1,0:T(8,128)(2,1)S(1)}, u32[]{:S(2)}) copy-start(bf16[8,96,256]{2,1,0:T(8,128)(2,1)S(1)} %all-to-all-done.2) | copy-start | bytes 1179652
  120.6 69.6 %collective-permute-start.21 = (bf16[768,1536]{1,0:T(8,128)(2,1)}, bf16[768,1536]{1,0:T(8,128)(2,1)}, u32[]{:S(2)}, u32[]{:S(2)}) collective-permute-start(bf16[768,1536]{1,0:T(8,128)(2,1)} %slice.379.feed0), channel_id=1, source_target_pairs={{0,2},{1,3},{2,0},{3,1},{4,6},{5,7},{6,4},{7,5},{8,10},{9,11},{10,... | collective-permute-start | bytes 7077896 | tf_op jit(solution)/shard_map/ppermute | solution.py:44
  123.9 20.6 %copy-start.32 = (f32[32,24]{1,0:T(8,128)}, f32[32,24]{1,0:T(8,128)S(1)}, u32[]{:S(2)}) copy-start(f32[32,24]{1,0:T(8,128)S(1)} %get-tuple-element.256) | copy-start | bytes 9220
  124.0 22.5 %collective-permute-start.17 = (bf16[768,768]{1,0:T(8,128)(2,1)S(1)}, bf16[768,768]{1,0:T(8,128)(2,1)}, u32[]{:S(2)}, u32[]{:S(2)}) collective-permute-start(bf16[768,768]{1,0:T(8,128)(2,1)S(1)} %slice.381.refs_1_.refs_5_), channel_id=1, source_target_pairs={{0,1},{1,0},{2,3},{3,2},{4,5},{5,4},{6,7},{7,6},{8,9},{9,8},{10,11... | collective-permute-start | bytes 3538952 | tf_op jit(solution)/shard_map/ppermute | solution.py:44
  141.0 5.5 %collective-permute-start.19 = (bf16[768,768]{1,0:T(8,128)(2,1)S(1)}, bf16[768,768]{1,0:T(8,128)(2,1)}, u32[]{:S(2)}, u32[]{:S(2)}) collective-permute-start(bf16[768,768]{1,0:T(8,128)(2,1)S(1)} %collective-permute-done.18.refs_3_.refs_7_), channel_id=1, source_target_pairs={{0,1},{1,0},{2,3},{3,2},{4,5},{5,4},{6,7},{7,6},{8,9},{9,8},{10,11... | collective-permute-start | bytes 3538952 | tf_op jit(solution)/shard_map/ppermute | solution.py:44
  151.5 38.6 %copy-start.40 = (s32[2,12]{1,0:T(2,128)S(1)}, s32[2,12]{1,0:T(2,128)}, u32[]{:S(2)}) copy-start(s32[2,12]{1,0:T(2,128)} %copy-done.39) | copy-start | bytes 292
  151.5 47.4 %all-to-all-start.3 = ((bf16[8,576,128]{2,1,0:T(8,128)(2,1)}), bf16[8,576,128]{2,1,0:T(8,128)(2,1)S(1)}, u32[]{:S(2)}, u32[]{:S(2)}) async-start(bf16[8,576,128]{2,1,0:T(8,128)(2,1)} %head_projection.1), calls=%async_computation.3 | async-start | bytes 2359296 | tf_op jit(solution)/shard_map/all_to_all | solution.py:695
  157.9 59.6 %collective-permute-start.20 = (bf16[768,1536]{1,0:T(8,128)(2,1)}, bf16[768,1536]{1,0:T(8,128)(2,1)}, u32[]{:S(2)}, u32[]{:S(2)}) collective-permute-start(bf16[768,1536]{1,0:T(8,128)(2,1)} %slice.379.feed0), channel_id=1, source_target_pairs={{0,1},{1,0},{2,3},{3,2},{4,5},{5,4},{6,7},{7,6},{8,9},{9,8},{10,11... | collective-permute-start | bytes 7077896 | tf_op jit(solution)/shard_map/ppermute | solution.py:44
  190.1 27.4 %collective-permute-start.22 = (bf16[768,1536]{1,0:T(8,128)(2,1)}, bf16[768,1536]{1,0:T(8,128)(2,1)}, u32[]{:S(2)}, u32[]{:S(2)}) collective-permute-start(bf16[768,1536]{1,0:T(8,128)(2,1)} %collective-permute-done.21.feed2), channel_id=1, source_target_pairs={{0,1},{1,0},{2,3},{3,2},{4,5},{5,4},{6,7},{7,6},{8,9},{9,8},{10,11... | collective-permute-start | bytes 7077896 | tf_op jit(solution)/shard_map/ppermute | solution.py:44
  206.4 9.3 %copy-start.34 = (f32[32,24]{1,0:T(8,128)S(1)}, f32[32,24]{1,0:T(8,128)}, u32[]{:S(2)}) copy-start(f32[32,24]{1,0:T(8,128)} %get-tuple-element.254) | copy-start | bytes 9220
  206.4 9.9 %copy-start.12 = (f32[256,768]{0,1:T(8,128)S(1)}, f32[256,768]{0,1:T(8,128)}, u32[]{:S(2)}) copy-start(f32[256,768]{0,1:T(8,128)} %get-tuple-element.187) | copy-start | bytes 2359300
  208.5 16.4 %all-to-all-start.4 = ((bf16[8,192,128]{2,1,0:T(8,128)(2,1)}), bf16[8,192,128]{2,1,0:T(8,128)(2,1)S(1)}, u32[]{:S(2)}, u32[]{:S(2)}) async-start(bf16[8,192,128]{2,1,0:T(8,128)(2,1)} %convert_element_type.257), calls=%async_computation.4 | async-start | bytes 786432 | tf_op jit(solution)/shard_map/all_to_all | solution.py:695
  238.2 15.8 %all-to-all-start.5 = ((bf16[8,192,128]{2,1,0:T(8,128)(2,1)}), bf16[8,192,128]{2,1,0:T(8,128)(2,1)S(1)}, u32[]{:S(2)}, u32[]{:S(2)}) async-start(bf16[8,192,128]{2,1,0:T(8,128)(2,1)} %get-tuple-element.68), calls=%async_computation.5 | async-start | bytes 786432 | tf_op jit(solution)/shard_map/all_to_all | solution.py:695
  272.7 31.6 %all-to-all-start.6 = ((bf16[8,3,192,128]{3,2,1,0:T(8,128)(2,1)}), bf16[8,3,192,128]{3,2,1,0:T(8,128)(2,1)S(1)}, u32[]{:S(2)}, u32[]{:S(2)}) async-start(bf16[8,3,192,128]{3,2,1,0:T(8,128)(2,1)} %copy.228), calls=%async_computation.6 | async-start | bytes 2359296 | tf_op jit(solution)/shard_map/all_to_all | solution.py:695
  278.8 208.4 %reduce-scatter.2.cloned.1.call-start = ((), (), s32[]{:S(2)}) async-start(), calls=%async_computation.14 | async-start | bytes 9732096 | tf_op jit(solution)/shard_map/reduce_scatter | solution.py:845
  306.5 18.6 %collective-permute-start.24 = (bf16[768,768]{0,1:T(8,128)(2,1)}, bf16[768,768]{0,1:T(8,128)(2,1)}, u32[]{:S(2)}, u32[]{:S(2)}) collective-permute-start(bf16[768,768]{0,1:T(8,128)(2,1)} %pad_maximum_fusion.5), channel_id=1, source_target_pairs={{0,1},{1,0},{2,3},{3,2},{4,5},{5,4},{6,7},{7,6},{8,9},{9,8},{10,11... | collective-permute-start | bytes 3538952 | tf_op jit(solution)/shard_map/ppermute | solution.py:44
  308.4 19.4 %collective-permute-start.23 = (bf16[768,768]{0,1:T(8,128)(2,1)}, bf16[768,768]{0,1:T(8,128)(2,1)}, u32[]{:S(2)}, u32[]{:S(2)}) collective-permute-start(bf16[768,768]{0,1:T(8,128)(2,1)} %pad_maximum_fusion.4), channel_id=1, source_target_pairs={{0,1},{1,0},{2,3},{3,2},{4,5},{5,4},{6,7},{7,6},{8,9},{9,8},{10,11... | collective-permute-start | bytes 3538952 | tf_op jit(solution)/shard_map/ppermute | solution.py:44
  317.0 16.7 %all-to-all-start.7 = ((bf16[8,96,256]{2,1,0:T(8,128)(2,1)}), bf16[8,96,256]{2,1,0:T(8,128)(2,1)S(1)}, u32[]{:S(2)}, u32[]{:S(2)}) async-start(bf16[8,96,256]{2,1,0:T(8,128)(2,1)} %bitcast.394), calls=%async_computation.7 | async-start | bytes 786432 | tf_op jit(solution)/shard_map/all_to_all | solution.py:695
  329.4 24.1 %copy-start.15 = (bf16[256,1024]{1,0:T(8,128)(2,1)S(1)}, bf16[256,1024]{1,0:T(8,128)(2,1)}, u32[]{:S(2)}) copy-start(bf16[256,1024]{1,0:T(8,128)(2,1)} %concatenate.67) | copy-start | bytes 1572868
  329.4 24.1 %copy-start.24 = (bf16[256,512]{1,0:T(8,128)(2,1)S(1)}, bf16[256,512]{1,0:T(8,128)(2,1)}, u32[]{:S(2)}) copy-start(bf16[256,512]{1,0:T(8,128)(2,1)} %bitcast_multiply_fusion) | copy-start | bytes 786436
  333.7 36.4 %collective-permute-start.25 = (bf16[768,768]{0,1:T(8,128)(2,1)}, bf16[768,768]{0,1:T(8,128)(2,1)}, u32[]{:S(2)}, u32[]{:S(2)}) collective-permute-start(bf16[768,768]{0,1:T(8,128)(2,1)} %add_convert_fusion.1), channel_id=1, source_target_pairs={{0,2},{1,3},{2,0},{3,1},{4,6},{5,7},{6,4},{7,5},{8,10},{9,11},{10,... | collective-permute-start | bytes 3538952 | tf_op jit(solution)/shard_map/ppermute | solution.py:44
  347.4 24.4 %all-to-all-start.8 = ((bf16[8,96,256]{2,1,0:T(8,128)(2,1)}), bf16[8,96,256]{2,1,0:T(8,128)(2,1)S(1)}, u32[]{:S(2)}, u32[]{:S(2)}) async-start(bf16[8,96,256]{2,1,0:T(8,128)(2,1)} %get-tuple-element.81), calls=%async_computation.8 | async-start | bytes 786432 | tf_op jit(solution)/shard_map/all_to_all | solution.py:695
  381.4 9.7 %collective-permute-start.28 = (bf16[8,80,512]{2,1,0:T(8,128)(2,1)S(1)}, bf16[8,80,512]{2,1,0:T(8,128)(2,1)S(1)}, u32[]{:S(2)}, u32[]{:S(2)}) collective-permute-start(bf16[8,80,512]{2,1,0:T(8,128)(2,1)S(1)} %get-tuple-element.204), channel_id=1, source_target_pairs={{0,1},{1,0},{2,3},{3,2},{4,5},{5,4},{6,7},{7,6},{8,9},{9,8},{10,11... | collective-permute-start | bytes 1966088 | tf_op jit(solution)/shard_map/ppermute | solution.py:44
  383.3 9.8 %copy-start.23 = (bf16[8,96,768]{2,1,0:T(8,128)(2,1)S(1)}, bf16[8,96,768]{2,1,0:T(8,128)(2,1)}, u32[]{:S(2)}) copy-start(bf16[8,96,768]{2,1,0:T(8,128)(2,1)} %get-tuple-element.92) | copy-start | bytes 3538948
  383.3 28.8 %all-to-all-start.9 = ((bf16[8,1,96,384]{3,2,1,0:T(8,128)(2,1)}), bf16[8,1,96,384]{3,2,1,0:T(8,128)(2,1)}, u32[]{:S(2)}, u32[]{:S(2)}) async-start(bf16[8,1,96,384]{3,2,1,0:T(8,128)(2,1)} %bitcast.89), calls=%async_computation.9 | async-start | bytes 1179648 | tf_op jit(solution)/shard_map/all_to_all | solution.py:695
  395.7 16.5 %copy-start.14 = (bf16[768,384]{0,1:T(8,128)(2,1)S(1)}, bf16[768,384]{0,1:T(8,128)(2,1)}, u32[]{:S(2)}) copy-start(bf16[768,384]{0,1:T(8,128)(2,1)} %get-tuple-element.94) | copy-start | bytes 1769476
  395.7 2.2 collective-permute-start.31
  395.7 27.2 %collective-permute-start.30 = (bf16[1,8,96,192]{3,2,1,0:T(8,128)(2,1)}, bf16[1,8,96,192]{3,2,1,0:T(8,128)(2,1)}, u32[]{:S(2)}, u32[]{:S(2)}) collective-permute-start(bf16[1,8,96,192]{3,2,1,0:T(8,128)(2,1)} %get-tuple-element.209), channel_id=1, source_target_pairs={{0,1},{1,0},{2,3},{3,2},{4,5},{5,4},{6,7},{7,6},{8,9},{9,8},{10,11... | collective-permute-start | bytes 884744 | tf_op jit(solution)/shard_map/ppermute | solution.py:44
  398.9 24.0 %collective-permute-start.32 = (bf16[1,8,96,192]{3,2,1,0:T(8,128)(2,1)}, bf16[1,8,96,192]{3,2,1,0:T(8,128)(2,1)}, u32[]{:S(2)}, u32[]{:S(2)}) collective-permute-start(bf16[1,8,96,192]{3,2,1,0:T(8,128)(2,1)} %fusion.37), channel_id=1, source_target_pairs={{0,2},{1,3},{2,0},{3,1},{4,6},{5,7},{6,4},{7,5},{8,10},{9,11},{10,... | collective-permute-start | bytes 884744 | tf_op jit(solution)/shard_map/ppermute | solution.py:44
  399.7 24.8 %collective-permute-start.27 = (bf16[8,80,512]{2,1,0:T(8,128)(2,1)S(1)}, bf16[8,80,512]{2,1,0:T(8,128)(2,1)S(1)}, u32[]{:S(2)}, u32[]{:S(2)}) collective-permute-start(bf16[8,80,512]{2,1,0:T(8,128)(2,1)S(1)} %copy-done.25), channel_id=1, source_target_pairs={{0,1},{1,0},{2,3},{3,2},{4,5},{5,4},{6,7},{7,6},{8,9},{9,8},{10,11... | collective-permute-start | bytes 1966088 | tf_op jit(solution)/shard_map/ppermute | solution.py:44
  399.7 24.8 %collective-permute-start.29 = (bf16[8,80,512]{2,1,0:T(8,128)(2,1)}, bf16[8,80,512]{2,1,0:T(8,128)(2,1)}, u32[]{:S(2)}, u32[]{:S(2)}) collective-permute-start(bf16[8,80,512]{2,1,0:T(8,128)(2,1)} %fusion), channel_id=1, source_target_pairs={{0,2},{1,3},{2,0},{3,1},{4,6},{5,7},{6,4},{7,5},{8,10},{9,11},{10,... | collective-permute-start | bytes 1966088 | tf_op jit(solution)/shard_map/ppermute | solution.py:44
  413.2 28.7 %all-to-all-start.10 = ((bf16[8,1,96,384]{3,2,1,0:T(8,128)(2,1)}), bf16[8,1,96,384]{3,2,1,0:T(8,128)(2,1)S(1)}, u32[]{:S(2)}, u32[]{:S(2)}) async-start(bf16[8,1,96,384]{3,2,1,0:T(8,128)(2,1)} %bitcast.91), calls=%async_computation.10 | async-start | bytes 1179648 | tf_op jit(solution)/shard_map/all_to_all | solution.py:695
  442.0 41.4 %all-to-all-start.11 = ((bf16[8,1,128,512]{3,2,1,0:T(8,128)(2,1)}), bf16[8,1,128,512]{3,2,1,0:T(8,128)(2,1)S(1)}, u32[]{:S(2)}, u32[]{:S(2)}) async-start(bf16[8,1,128,512]{3,2,1,0:T(8,128)(2,1)} %bitcast.93), calls=%async_computation.11 | async-start | bytes 2097152 | tf_op jit(solution)/shard_map/all_to_all | solution.py:695
  449.8 23.4 %collective-permute-start.26 = (f32[2,1,512]{2,1,0:T(1,128)S(1)}, f32[2,1,512]{2,1,0:T(1,128)S(1)}, u32[]{:S(2)}, u32[]{:S(2)}) collective-permute-start(f32[2,1,512]{2,1,0:T(1,128)S(1)} %slice.405), channel_id=1, source_target_pairs={{0,4},{4,8},{8,12},{12,16},{16,20},{20,24},{24,28},{1,5},{5,9},{9,... | collective-permute-start | bytes 12296 | tf_op jit(solution)/shard_map/ppermute | solution.py:34
  475.9 4.3 collective-permute-start.33
  476.0 4.2 collective-permute-start.35
  476.1 5.6 %collective-permute-start.34 = (f32[24,576]{1,0:T(8,128)S(1)}, f32[24,576]{1,0:T(8,128)S(1)}, u32[]{:S(2)}, u32[]{:S(2)}) collective-permute-start(f32[24,576]{1,0:T(8,128)S(1)} %get-tuple-element.179), channel_id=1, source_target_pairs={{0,2},{1,3},{2,0},{3,1},{4,6},{5,7},{6,4},{7,5},{8,10},{9,11},{10,... | collective-permute-start | bytes 165896 | tf_op jit(solution)/shard_map/ppermute | solution.py:44
  (32 other events, 100.1 us)
Sparse Core Ops, SparseCore 0:
  24.3 78.1 all-gather.1
  285.6 156.9 reduce-scatter.1
